TPU v7x, 512 devices: a whole 4x4x16 slice. The times are simulated.
512 devices in a mesh: node: 16 (over z), local: 8 (over x, core), dp: 4 (over y).
Axes of the slice: x: 4, y: 4, z: 16, core: 2. Of those that a mesh axis runs over, the one named last changes fastest.
Arguments:
- layer_input: bfloat16 [8192, 2560], P(('node', 'dp'), 'local'), may hold values from -6 to 6
- grad_out: bfloat16 [8192, 2560], P(('node', 'dp'), 'local'), may hold values from -6 to 6
- gate_values: bfloat16 [8192, 6], P(('node', 'dp')), may hold values from 0.049804688 to 0.5
- route_expert: int32 [8192, 6], P(('node', 'dp')), may hold values from 0 to 159, as said below
- route_slot: int32 [8192, 6], P(('node', 'dp')), may hold values from -1 to 5, as said below
- shared_gate: bfloat16 [1536, 2560], P('local', 'dp'), may hold values from -0.125 to 0.125
- shared_up: bfloat16 [1536, 2560], P('local', 'dp'), may hold values from -0.125 to 0.125
- shared_down: bfloat16 [1536, 2560], P('local', 'dp'), may hold values from -0.15625 to 0.15625
- expert_gate: bfloat16 [64, 768, 2560], P(('node', 'dp'), 'local'), may hold values from -0.125 to 0.125
- expert_up: bfloat16 [64, 768, 2560], P(('node', 'dp'), 'local'), may hold values from -0.125 to 0.125
- expert_down: bfloat16 [64, 768, 2560], P(('node', 'dp'), 'local'), may hold values from -0.21875 to 0.21875
Outputs:
- grad_x: bfloat16 [8192, 2560], P(('node', 'dp'), 'local')
- grad_gates: float32 [8192, 6], P(('node', 'dp'))
- grad_shared_gate: bfloat16 [1536, 2560], P('local', 'dp')
- grad_shared_up: bfloat16 [1536, 2560], P('local', 'dp')
- grad_shared_down: bfloat16 [1536, 2560], P('local', 'dp')
- grad_expert_gate: bfloat16 [64, 768, 2560], P(('node', 'dp'), 'local')
- grad_expert_up: bfloat16 [64, 768, 2560], P(('node', 'dp'), 'local')
- grad_expert_down: bfloat16 [64, 768, 2560], P(('node', 'dp'), 'local')
Inputs may be any that keep to these rules, and one draw needn't show every extreme that they name: `route_expert`: each row names 6 different experts, all on at most 3 nodes; expert i lies on node i // 10. `route_slot`: for the choice of expert i, counting the choices of the 128 tokens of one group to the same expert in the order of rows, then of columns, from 0: the slot is that count, and it is -1 exactly where i % 10 >= 4 or the count reaches 6.
All inputs are finite; a program needn't handle non-finite values.
Results may differ from a plain program's by a relative error of at most 0.025.
Values may be sent and summed in bfloat16 or wider, within the bound.
A program may use at most 128 MiB of HBM per device.

v0:
```python
import jax
import jax.numpy as jnp
from jax import lax
from jax.sharding import PartitionSpec as P

NODE_EXPERTS = 10
CAP = 6


def contract_rows(left, right):
    return lax.dot_general(
        left, right, (((0,), (0,)), ((), ())), preferred_element_type=jnp.float32
    )


def contract_cols(left, right):
    return lax.dot_general(
        left, right, (((1,), (1,)), ((), ())), preferred_element_type=jnp.float32
    )


def on_device(
    layer_input,
    grad_out,
    gate_values,
    route_expert,
    route_slot,
    shared_gate,
    shared_up,
    shared_down,
    expert_gate,
    expert_up,
    expert_down,
):
    n_node = lax.axis_size("node")
    n_dp = lax.axis_size("dp")
    groups = n_node * n_dp
    feat_slice = layer_input.shape[1]
    slot_count = groups * CAP
    full_x, full_dy = (
        lax.all_gather(layer_input, "local", axis=1, tiled=True),
        lax.all_gather(grad_out, "local", axis=1, tiled=True),
    )
    kept = route_slot >= 0
    held = route_expert // NODE_EXPERTS * n_dp + route_expert % NODE_EXPERTS
    position = jnp.where(kept, held * CAP + route_slot, -1)
    slot_ids = jnp.arange(slot_count, dtype=jnp.int32)
    matches = position[None, :, :] == slot_ids[:, None, None]
    select = jnp.any(matches, axis=2).astype(jnp.bfloat16)
    slot_gate = jnp.sum(
        jnp.where(matches, gate_values.astype(jnp.float32)[None, :, :], 0.0), axis=(1, 2)
    ).astype(jnp.bfloat16)
    send_x = jnp.dot(select, full_x, preferred_element_type=jnp.float32).astype(jnp.bfloat16)
    send_dy = jnp.dot(select, full_dy, preferred_element_type=jnp.float32).astype(jnp.bfloat16)
    row_width = send_x.shape[1]
    recv_x, recv_dy, recv_gate = (
        lax.all_to_all(
            send_x.reshape(groups, CAP, row_width),
            ("node", "dp"),
            split_axis=0,
            concat_axis=0,
            tiled=True,
        ),
        lax.all_to_all(
            send_dy.reshape(groups, CAP, row_width),
            ("node", "dp"),
            split_axis=0,
            concat_axis=0,
            tiled=True,
        ),
        lax.all_to_all(
            slot_gate.reshape(groups, CAP), ("node", "dp"), split_axis=0, concat_axis=0, tiled=True
        ),
    )
    model_width = recv_x.shape[2]
    rows_x = recv_x.reshape(slot_count, model_width)
    rows_dy = recv_dy.reshape(slot_count, model_width)
    weight_q = recv_gate.reshape(slot_count).astype(jnp.float32)[:, None]
    weight_gate = expert_gate[0]
    weight_up = expert_up[0]
    weight_down = expert_down[0]
    feature_gate, feature_up = (
        lax.all_to_all(weight_gate, "local", split_axis=1, concat_axis=0, tiled=True),
        lax.all_to_all(weight_up, "local", split_axis=1, concat_axis=0, tiled=True),
    )
    pre_a = contract_cols(rows_x, weight_gate)
    pre_b = contract_cols(rows_x, weight_up)
    back_e = contract_cols(rows_dy, weight_down)
    sigm_a = jax.nn.sigmoid(pre_a)
    silu_a = pre_a * sigm_a
    hidden = silu_a * pre_b
    gate_part = jnp.sum(back_e * hidden, axis=1).reshape(groups, CAP)
    gate_grad = lax.psum(gate_part, "local")
    grad_a = (weight_q * back_e * pre_b * sigm_a * (1.0 + pre_a * (1.0 - sigm_a))).astype(
        jnp.bfloat16
    )
    grad_b = (weight_q * back_e * silu_a).astype(jnp.bfloat16)
    hidden_q = (weight_q * hidden).astype(jnp.bfloat16)
    new_gate = contract_rows(grad_a, rows_x).astype(jnp.bfloat16)
    new_up = contract_rows(grad_b, rows_x).astype(jnp.bfloat16)
    new_down = contract_rows(hidden_q, rows_dy).astype(jnp.bfloat16)
    total = jnp.dot(
        lax.all_gather(grad_a, "local", axis=1, tiled=True),
        feature_gate,
        preferred_element_type=jnp.float32,
    )
    row_dx = total + jnp.dot(
        lax.all_gather(grad_b, "local", axis=1, tiled=True),
        feature_up,
        preferred_element_type=jnp.float32,
    )
    back_dx, back_gate = (
        lax.all_to_all(
            row_dx.reshape(groups, CAP, feat_slice).astype(jnp.bfloat16),
            ("node", "dp"),
            split_axis=0,
            concat_axis=0,
            tiled=True,
        ).astype(jnp.float32),
        lax.all_to_all(
            gate_grad.astype(jnp.bfloat16), ("node", "dp"), split_axis=0, concat_axis=0, tiled=True
        ).astype(gate_grad.dtype),
    )
    back_rows = back_dx.reshape(slot_count, feat_slice)
    routed_dx = lax.dot_general(
        select.astype(jnp.float32),
        back_rows,
        (((0,), (0,)), ((), ())),
        precision=lax.Precision.HIGHEST,
        preferred_element_type=jnp.float32,
    )
    back_flat = back_gate.reshape(slot_count)
    grad_gates = jnp.sum(jnp.where(matches, back_flat[:, None, None], 0.0), axis=0)
    share_gate, share_up, share_down = (
        lax.all_gather(shared_gate, "dp", axis=1, tiled=True),
        lax.all_gather(shared_up, "dp", axis=1, tiled=True),
        lax.all_gather(shared_down, "dp", axis=1, tiled=True),
    )
    shared_a = contract_cols(full_x, share_gate)
    shared_b = contract_cols(full_x, share_up)
    shared_e = contract_cols(full_dy, share_down)
    sigm_s = jax.nn.sigmoid(shared_a)
    silu_s = shared_a * sigm_s
    shared_h = (silu_s * shared_b).astype(jnp.bfloat16)
    shared_da = (shared_e * shared_b * sigm_s * (1.0 + shared_a * (1.0 - sigm_s))).astype(
        jnp.bfloat16
    )
    shared_db = (shared_e * silu_s).astype(jnp.bfloat16)
    dx_part = jnp.dot(shared_da, share_gate, preferred_element_type=jnp.float32)
    dx_part = dx_part + jnp.dot(shared_db, share_up, preferred_element_type=jnp.float32)
    shared_dx = lax.psum_scatter(
        dx_part.astype(jnp.bfloat16), "local", scatter_dimension=1, tiled=True
    ).astype(jnp.float32)
    part_gate = contract_rows(shared_da, full_x)
    part_up = contract_rows(shared_db, full_x)
    part_down = contract_rows(shared_h, full_dy)
    sum_gate, sum_up, sum_down = (
        lax.psum_scatter(
            part_gate.astype(jnp.bfloat16), "dp", scatter_dimension=1, tiled=True
        ).astype(jnp.float32),
        lax.psum_scatter(
            part_up.astype(jnp.bfloat16), "dp", scatter_dimension=1, tiled=True
        ).astype(jnp.float32),
        lax.psum_scatter(
            part_down.astype(jnp.bfloat16), "dp", scatter_dimension=1, tiled=True
        ).astype(jnp.float32),
    )
    sum_gate, sum_up, sum_down = (
        lax.psum(sum_gate.astype(jnp.bfloat16), "node").astype(jnp.float32),
        lax.psum(sum_up.astype(jnp.bfloat16), "node").astype(jnp.float32),
        lax.psum(sum_down.astype(jnp.bfloat16), "node").astype(jnp.float32),
    )
    grad_x = (shared_dx + routed_dx).astype(jnp.bfloat16)
    return (
        grad_x,
        grad_gates,
        sum_gate.astype(jnp.bfloat16),
        sum_up.astype(jnp.bfloat16),
        sum_down.astype(jnp.bfloat16),
        new_gate[None],
        new_up[None],
        new_down[None],
    )


def solution(mesh):
    in_specs = (
        P(("node", "dp"), "local"),
        P(("node", "dp"), "local"),
        P(("node", "dp"), None),
        P(("node", "dp"), None),
        P(("node", "dp"), None),
        P("local", "dp"),
        P("local", "dp"),
        P("local", "dp"),
        P(("node", "dp"), "local", None),
        P(("node", "dp"), "local", None),
        P(("node", "dp"), "local", None),
    )
    out_specs = (
        P(("node", "dp"), "local"),
        P(("node", "dp"), None),
        P("local", "dp"),
        P("local", "dp"),
        P("local", "dp"),
        P(("node", "dp"), "local", None),
        P(("node", "dp"), "local", None),
        P(("node", "dp"), "local", None),
    )
    return jax.shard_map(
        on_device, mesh=mesh, in_specs=in_specs, out_specs=out_specs, check_vma=False
    )
```

profile of v0, /device:TPU:6, one launch (start us, length us, event | category | flops | bytes accessed | tf_op | source)
XLA Modules:
  0.0 593.0 jit_solution(10177772624062360092)
XLA Ops:
  8.1 16.6 %all_gather.23 = bf16[128,2560]{0,1:T(8,128)(2,1)S(1)} all-gather(bf16[128,320]{0,1:T(8,128)(2,1)} %param.11), channel_id=1, replica_groups=mesh['node'=16,'local'=8,'dp'=4] {'local'}, dimensions={1}, use_global_device_ids=true | all-gather | bytes 737280 | tf_op jit(solution)/shard_map/all_gather | solution.py:41
  24.7 2.0 convolution_convert_fusion
  26.7 4.1 reshape.81
  30.8 16.0 %all-to-all-start.2 = ((bf16[64,6,2560]{2,1,0:T(8,128)(2,1)}), bf16[64,6,2560]{2,1,0:T(8,128)(2,1)}, u32[]{:S(2)}, u32[]{:S(2)}) async-start(bf16[64,6,2560]{2,1,0:T(8,128)(2,1)} %reshape.81), calls=%async_computation.3 | async-start | bytes 5242880 | tf_op jit(solution)/shard_map/all_to_all | solution.py:57
  46.8 13.2 %all_gather.21 = bf16[128,2560]{0,1:T(8,128)(2,1)S(1)} all-gather(bf16[128,320]{0,1:T(8,128)(2,1)S(1)} %copy-done.24), channel_id=1, replica_groups=mesh['node'=16,'local'=8,'dp'=4] {'local'}, dimensions={1}, use_global_device_ids=true | all-gather | bytes 737280 | tf_op jit(solution)/shard_map/all_gather | solution.py:42
  60.0 2.0 convolution_convert_fusion.1
  62.1 4.1 reshape.79
  66.2 103.7 %all-to-all-done.2 = bf16[64,6,2560]{2,1,0:T(8,128)(2,1)} async-done(((bf16[64,6,2560]{2,1,0:T(8,128)(2,1)}), bf16[64,6,2560]{2,1,0:T(8,128)(2,1)}, u32[]{:S(2)}, u32[]{:S(2)}) %all-to-all-start.2) | async-done | bytes 1966112 | tf_op jit(solution)/shard_map/all_to_all | solution.py:57
  169.9 6.1 %all-to-all-start.1 = ((bf16[64,6,2560]{2,1,0:T(8,128)(2,1)}), bf16[64,6,2560]{2,1,0:T(8,128)(2,1)}, u32[]{:S(2)}, u32[]{:S(2)}) async-start(bf16[64,6,2560]{2,1,0:T(8,128)(2,1)} %reshape.79), calls=%async_computation.2 | async-start | bytes 5242880 | tf_op jit(solution)/shard_map/all_to_all | solution.py:64
  176.0 17.9 %all_gather.25 = bf16[192,2560]{1,0:T(8,128)(2,1)S(1)} all-gather(bf16[192,640]{1,0:T(8,128)(2,1)S(1)} %copy-done.21), channel_id=1, replica_groups=mesh['node'=16,'local'=8,'dp'=4] {'dp'}, dimensions={1}, use_global_device_ids=true | all-gather | bytes 1228800 | tf_op jit(solution)/shard_map/all_gather | solution.py:135
  194.3 17.8 %all_gather.24 = bf16[192,2560]{1,0:T(8,128)(2,1)S(1)} all-gather(bf16[192,640]{1,0:T(8,128)(2,1)S(1)} %copy-done.22), channel_id=1, replica_groups=mesh['node'=16,'local'=8,'dp'=4] {'dp'}, dimensions={1}, use_global_device_ids=true | all-gather | bytes 1228800 | tf_op jit(solution)/shard_map/all_gather | solution.py:136
  213.9 2.5 copy.42
  216.6 17.0 %all_gather.22 = bf16[192,2560]{1,0:T(8,128)(2,1)S(1)} all-gather(bf16[192,640]{1,0:T(8,128)(2,1)S(1)} %copy-done.23), channel_id=1, replica_groups=mesh['node'=16,'local'=8,'dp'=4] {'dp'}, dimensions={1}, use_global_device_ids=true | all-gather | bytes 1228800 | tf_op jit(solution)/shard_map/all_gather | solution.py:137
  237.7 2.8 reshape.82
  240.5 57.5 %all-to-all-done.1 = bf16[64,6,2560]{2,1,0:T(8,128)(2,1)} async-done(((bf16[64,6,2560]{2,1,0:T(8,128)(2,1)}), bf16[64,6,2560]{2,1,0:T(8,128)(2,1)}, u32[]{:S(2)}, u32[]{:S(2)}) %all-to-all-start.1) | async-done | bytes 1966112 | tf_op jit(solution)/shard_map/all_to_all | solution.py:64
  298.0 4.2 reshape.80
  307.1 21.3 %psum.28 = bf16[64,6]{1,0:T(8,128)(2,1)S(1)} all-reduce(f32[64,6]{1,0:T(8,128)} %reshape.84), channel_id=1, replica_groups=mesh['node'=16,'local'=8,'dp'=4] {'local'}, use_global_device_ids=true, to_apply=%region_4.5 | all-reduce | flops 384 | bytes 2304 | tf_op jit(solution)/shard_map/psum | solution.py:93
  329.0 6.6 %all-to-all-start.6 = ((bf16[64,1,6]{2,1,0:T(2,128)(2,1)}), bf16[64,1,6]{2,1,0:T(2,128)(2,1)}, u32[]{:S(2)}, u32[]{:S(2)}) async-start(bf16[64,1,6]{2,1,0:T(2,128)(2,1)} %copy.37), calls=%async_computation.7 | async-start | bytes 65536 | tf_op jit(solution)/shard_map/all_to_all | solution.py:120
  335.7 2.9 fusion.26
  338.6 11.7 %all-to-all-done.6 = bf16[64,1,6]{2,1,0:T(2,128)(2,1)} async-done(((bf16[64,1,6]{2,1,0:T(2,128)(2,1)}), bf16[64,1,6]{2,1,0:T(2,128)(2,1)}, u32[]{:S(2)}, u32[]{:S(2)}) %all-to-all-start.6) | async-done | bytes 800 | tf_op jit(solution)/shard_map/all_to_all | solution.py:120
  353.0 5.4 all-to-all-start
  358.5 2.8 fusion
  361.4 2.4 all_to_all.50
  364.2 2.0 copy.34
  367.1 5.7 all-to-all-done
  372.8 7.7 %all-to-all-start.3 = ((bf16[96,8,320]{2,0,1:T(8,128)(2,1)}), bf16[96,8,320]{2,0,1:T(8,128)(2,1)S(1)}, u32[]{:S(2)}, u32[]{:S(2)}) async-start(bf16[96,8,320]{2,0,1:T(8,128)(2,1)} %copy.34), calls=%async_computation.4 | async-start | bytes 1179648 | tf_op jit(solution)/shard_map/all_to_all | solution.py:83
  383.1 16.3 %all_gather.26 = bf16[384,768]{0,1:T(8,128)(2,1)} all-gather(bf16[384,96]{0,1:T(8,128)(2,1)S(1)} %get-tuple-element.14), channel_id=1, replica_groups=mesh['node'=16,'local'=8,'dp'=4] {'local'}, dimensions={1}, use_global_device_ids=true | all-gather | bytes 663552 | tf_op jit(solution)/shard_map/all_gather | solution.py:103
  399.4 5.6 all-to-all-start.4
  404.9 17.6 %all_gather.27 = bf16[384,768]{0,1:T(8,128)(2,1)} all-gather(bf16[384,96]{0,1:T(8,128)(2,1)S(1)} %get-tuple-element.13), channel_id=1, replica_groups=mesh['node'=16,'local'=8,'dp'=4] {'local'}, dimensions={1}, use_global_device_ids=true | all-gather | bytes 663552 | tf_op jit(solution)/shard_map/all_gather | solution.py:108
  427.0 9.1 %all-to-all-start.5 = ((bf16[64,6,320]{2,1,0:T(8,128)(2,1)}), bf16[64,6,320]{2,1,0:T(8,128)(2,1)S(1)}, u32[]{:S(2)}, u32[]{:S(2)}) async-start(bf16[64,6,320]{2,1,0:T(8,128)(2,1)} %convert_element_type.126), calls=%async_computation.6 | async-start | bytes 786432 | tf_op jit(solution)/shard_map/all_to_all | solution.py:113
  445.6 18.2 %all-to-all-done.5 = bf16[64,6,320]{2,1,0:T(8,128)(2,1)S(1)} async-done(((bf16[64,6,320]{2,1,0:T(8,128)(2,1)}), bf16[64,6,320]{2,1,0:T(8,128)(2,1)S(1)}, u32[]{:S(2)}, u32[]{:S(2)}) %all-to-all-start.5) | async-done | bytes 245792 | tf_op jit(solution)/shard_map/all_to_all | solution.py:113
  465.8 115.7 %all-reduce.3.cloned.1.call-done = (bf16[192,640]{1,0:T(8,128)(2,1)}, bf16[192,640]{1,0:T(8,128)(2,1)}, bf16[192,640]{1,0:T(8,128)(2,1)}) async-done(((bf16[192,640]{1,0:T(8,128)(2,1)}, bf16[192,640]{1,0:T(8,128)(2,1)}, bf16[192,640]{1,0:T(8,128)(2,1)}), (bf16[192,640]{1,0:T(8,128)(2,1)}, bf16[192,640]{1,0:T(8,128)(2,1)}, bf16[192,640]{1,0:T(8,128)(2,1)})) %all-reduce.3.cloned.1.call-update) | async-done | bytes 737296 | tf_op jit(solution)/shard_map/psum | solution.py:169
  (112 shorter events, 40.3 us)
Async XLA Ops:
  7.2 297.7 %copy-start = (bf16[1,96,2560]{2,1,0:T(8,128)(2,1)S(1)}, bf16[1,96,2560]{2,1,0:T(8,128)(2,1)}, u32[]{:S(2)}) copy-start(bf16[1,96,2560]{2,1,0:T(8,128)(2,1)} %param.21) | copy-start | bytes 1474564
  8.0 18.7 %copy-start.25 = (s32[128,6]{0,1:T(8,128)}, s32[128,6]{0,1:T(8,128)S(1)}, u32[]{:S(2)}) copy-start(s32[128,6]{0,1:T(8,128)S(1)} %fusion.22) | copy-start | bytes 9220
  8.1 51.9 %copy-start.15 = (pred[384,128]{1,0:T(8,128)(4,1)}, pred[384,128]{1,0:T(8,128)(4,1)S(1)}, u32[]{:S(2)}) copy-start(pred[384,128]{1,0:T(8,128)(4,1)S(1)} %fusion.5) | copy-start | bytes 147460
  30.8 16.0 %copy-start.24 = (bf16[128,320]{0,1:T(8,128)(2,1)S(1)}, bf16[128,320]{0,1:T(8,128)(2,1)}, u32[]{:S(2)}) copy-start(bf16[128,320]{0,1:T(8,128)(2,1)} %param.12) | copy-start | bytes 245764
  30.8 139.1 %all-to-all-start.2 = ((bf16[64,6,2560]{2,1,0:T(8,128)(2,1)}), bf16[64,6,2560]{2,1,0:T(8,128)(2,1)}, u32[]{:S(2)}, u32[]{:S(2)}) async-start(bf16[64,6,2560]{2,1,0:T(8,128)(2,1)} %reshape.81), calls=%async_computation.3 | async-start | bytes 5242880 | tf_op jit(solution)/shard_map/all_to_all | solution.py:57
  60.0 6.2 %copy-start.4 = (bf16[128,2560]{0,1:T(8,128)(2,1)}, bf16[128,2560]{0,1:T(8,128)(2,1)S(1)}, u32[]{:S(2)}) copy-start(bf16[128,2560]{0,1:T(8,128)(2,1)S(1)} %all_gather.21) | copy-start | bytes 1966084
  66.2 109.8 %copy-start.21 = (bf16[192,640]{1,0:T(8,128)(2,1)S(1)}, bf16[192,640]{1,0:T(8,128)(2,1)}, u32[]{:S(2)}) copy-start(bf16[192,640]{1,0:T(8,128)(2,1)} %param.16) | copy-start | bytes 737284
  169.9 128.2 %all-to-all-start.1 = ((bf16[64,6,2560]{2,1,0:T(8,128)(2,1)}), bf16[64,6,2560]{2,1,0:T(8,128)(2,1)}, u32[]{:S(2)}, u32[]{:S(2)}) async-start(bf16[64,6,2560]{2,1,0:T(8,128)(2,1)} %reshape.79), calls=%async_computation.2 | async-start | bytes 5242880 | tf_op jit(solution)/shard_map/all_to_all | solution.py:64
  175.9 260.2 %reduce-scatter.17.cloned.1.call-start = ((), (), s32[]{:S(2)}) async-start(), calls=%async_computation.14 | async-start | bytes 1638400
  176.0 18.3 %copy-start.22 = (bf16[192,640]{1,0:T(8,128)(2,1)S(1)}, bf16[192,640]{1,0:T(8,128)(2,1)}, u32[]{:S(2)}) copy-start(bf16[192,640]{1,0:T(8,128)(2,1)} %param.17) | copy-start | bytes 737284
  193.9 18.6 %copy-start.1 = (bf16[192,2560]{1,0:T(8,128)(2,1)}, bf16[192,2560]{1,0:T(8,128)(2,1)S(1)}, u32[]{:S(2)}) copy-start(bf16[192,2560]{1,0:T(8,128)(2,1)S(1)} %all_gather.25) | copy-start | bytes 2949124
  193.9 18.6 %copy-start.5 = (bf16[128,2560]{0,1:T(8,128)(2,1)S(1)}, bf16[128,2560]{0,1:T(8,128)(2,1)}, u32[]{:S(2)}) copy-start(bf16[128,2560]{0,1:T(8,128)(2,1)} %copy-done.4) | copy-start | bytes 1966084
  213.9 19.6 %copy-start.6 = (bf16[128,2560]{0,1:T(8,128)(2,1)S(1)}, bf16[128,2560]{0,1:T(8,128)(2,1)}, u32[]{:S(2)}) copy-start(bf16[128,2560]{0,1:T(8,128)(2,1)} %copy-done.4) | copy-start | bytes 1966084
  216.5 221.4 %reduce-scatter.15.cloned.1.call-start = ((), (), s32[]{:S(2)}) async-start(), calls=%async_computation.13 | async-start | bytes 1638400
  235.8 204.0 %reduce-scatter.13.cloned.1.call-start = ((), (), s32[]{:S(2)}) async-start(), calls=%async_computation.12 | async-start | bytes 1638400
  302.2 2.7 copy-start.2
  329.0 9.6 %copy-start.27 = (bf16[128,6]{0,1:T(8,128)(2,1)S(1)}, bf16[128,6]{0,1:T(8,128)(2,1)}, u32[]{:S(2)}) copy-start(bf16[128,6]{0,1:T(8,128)(2,1)} %param.13) | copy-start | bytes 4612
  329.0 22.3 %copy-start.26 = (s32[128,6]{0,1:T(8,128)S(1)}, s32[128,6]{0,1:T(8,128)}, u32[]{:S(2)}) copy-start(s32[128,6]{0,1:T(8,128)} %copy-done.25) | copy-start | bytes 9220
  329.0 21.3 %all-to-all-start.6 = ((bf16[64,1,6]{2,1,0:T(2,128)(2,1)}), bf16[64,1,6]{2,1,0:T(2,128)(2,1)}, u32[]{:S(2)}, u32[]{:S(2)}) async-start(bf16[64,1,6]{2,1,0:T(2,128)(2,1)} %copy.37), calls=%async_computation.7 | async-start | bytes 65536 | tf_op jit(solution)/shard_map/all_to_all | solution.py:120
  353.0 19.8 %all-to-all-start = ((bf16[64,1,6]{2,1,0:T(2,128)(2,1)}), bf16[64,1,6]{2,1,0:T(2,128)(2,1)}, u32[]{:S(2)}, u32[]{:S(2)}) async-start(bf16[64,1,6]{2,1,0:T(2,128)(2,1)} %convert_element_type.141), calls=%async_computation.1 | async-start | bytes 65536 | tf_op jit(solution)/shard_map/all_to_all | solution.py:71
  358.5 105.5 %reduce-scatter.11.cloned.1.call-start = ((), (), s32[]{:S(2)}) async-start(), calls=%async_computation.11 | async-start | bytes 737280 | tf_op jit(solution)/shard_map/reduce_scatter | solution.py:151
  364.2 17.3 %copy-start.10 = (f32[384,96]{0,1:T(8,128)S(1)}, f32[384,96]{0,1:T(8,128)}, u32[]{:S(2)}) copy-start(f32[384,96]{0,1:T(8,128)} %copy-done.9) | copy-start | bytes 442372
  364.2 17.3 %copy-start.13 = (f32[384,96]{0,1:T(8,128)S(1)}, f32[384,96]{0,1:T(8,128)}, u32[]{:S(2)}) copy-start(f32[384,96]{0,1:T(8,128)} %copy-done.12) | copy-start | bytes 442372
  372.8 26.6 %all-to-all-start.3 = ((bf16[96,8,320]{2,0,1:T(8,128)(2,1)}), bf16[96,8,320]{2,0,1:T(8,128)(2,1)S(1)}, u32[]{:S(2)}, u32[]{:S(2)}) async-start(bf16[96,8,320]{2,0,1:T(8,128)(2,1)} %copy.34), calls=%async_computation.4 | async-start | bytes 1179648 | tf_op jit(solution)/shard_map/all_to_all | solution.py:83
  382.5 40.1 %copy-start.19 = (bf16[384,96]{0,1:T(8,128)(2,1)}, bf16[384,96]{0,1:T(8,128)(2,1)S(1)}, u32[]{:S(2)}) copy-start(bf16[384,96]{0,1:T(8,128)(2,1)S(1)} %get-tuple-element.13) | copy-start | bytes 221188
  399.4 24.8 %all-to-all-start.4 = ((bf16[96,8,320]{2,0,1:T(8,128)(2,1)}), bf16[96,8,320]{2,0,1:T(8,128)(2,1)}, u32[]{:S(2)}, u32[]{:S(2)}) async-start(bf16[96,8,320]{2,0,1:T(8,128)(2,1)} %copy.35), calls=%async_computation.5 | async-start | bytes 1179648 | tf_op jit(solution)/shard_map/all_to_all | solution.py:84
  426.1 15.6 %copy-start.20 = (bf16[384,96]{0,1:T(8,128)(2,1)S(1)}, bf16[384,96]{0,1:T(8,128)(2,1)}, u32[]{:S(2)}) copy-start(bf16[384,96]{0,1:T(8,128)(2,1)} %copy-done.19) | copy-start | bytes 221188
  427.0 36.8 %all-to-all-start.5 = ((bf16[64,6,320]{2,1,0:T(8,128)(2,1)}), bf16[64,6,320]{2,1,0:T(8,128)(2,1)S(1)}, u32[]{:S(2)}, u32[]{:S(2)}) async-start(bf16[64,6,320]{2,1,0:T(8,128)(2,1)} %convert_element_type.126), calls=%async_computation.6 | async-start | bytes 786432 | tf_op jit(solution)/shard_map/all_to_all | solution.py:113
  436.0 145.4 %all-reduce.3.cloned.1.call-start = ((), (), s32[]{:S(2)}) async-start(), calls=%async_computation.15 | async-start | bytes 1474560 | tf_op jit(solution)/shard_map/psum | solution.py:169
  439.8 3.2 copy-start.18
  441.6 2.6 copy-start.3
  444.3 19.7 %copy-start.16 = (pred[384,128]{1,0:T(8,128)(4,1)S(1)}, pred[384,128]{1,0:T(8,128)(4,1)}, u32[]{:S(2)}) copy-start(pred[384,128]{1,0:T(8,128)(4,1)} %copy-done.15) | copy-start | bytes 147460
  (8 other events, 16.4 us)
Sparse Core Ops, SparseCore 0:
  216.6 33.7 reduce-scatter.16
  253.3 36.2 reduce-scatter.14
  292.5 31.1 reduce-scatter.12
  361.8 40.6 reduce-scatter.10
  441.8 139.6 all-reduce.2
where the time goes:
time: 595 us; the launch traced here: 593 us
  waiting for transfers between devices  313 us (53%)
  blocking collectives  138 us (23%)
  starting transfers between devices  56.6 us (10%)
  local copies, waits for them, and re-layouts  41.1 us (7%)
  matrix products  26.2 us (4%)
  between operations  14.2 us (2%)
    psum x1, waiting for transfers between devices, on_device(): lax.psum(sum_gate.astype(jnp.bfloat16), 'node').astype(jnp.float32)  116 us
    all_to_all x1, waiting for transfers between devices, on_device(): lax.all_to_all(send_x.reshape(groups, CAP, row_width), ('node', 'dp'), sp...  104 us
    all_to_all x1, waiting for transfers between devices, on_device(): lax.all_to_all(send_dy.reshape(groups, CAP, row_width), ('node', 'dp'), s...  57.5 us
    psum x1, blocking collectives, on_device(): gate_grad = lax.psum(gate_part, 'local')  21.3 us
    all_to_all x1, waiting for transfers between devices, on_device(): lax.all_to_all(row_dx.reshape(groups, CAP, feat_slice).astype(jnp.bfloat1...  18.2 us
    all_gather x1, blocking collectives, on_device(): lax.all_gather(shared_gate, 'dp', axis=1, tiled=True)  17.9 us
    all_gather x1, blocking collectives, on_device(): lax.all_gather(shared_up, 'dp', axis=1, tiled=True)  17.8 us
    all_gather x1, blocking collectives, on_device(): lax.all_gather(grad_b, 'local', axis=1, tiled=True)  17.6 us
  transfers between devices with their start and end apart: 12, of which 6 were waited for; matrix products, arithmetic and copies ran while one was open for 9% of the time, Pallas kernels for 0%

commit v1 on v0

v1 whole, which is shorter than its diff:
```python
import jax
import jax.numpy as jnp
from jax import lax
from jax.experimental import pallas as pl
from jax.experimental.pallas import tpu as pltpu
from jax.sharding import PartitionSpec as P

BF = jnp.bfloat16
F32 = jnp.float32
MESH = pl.DeviceIdType.MESH


def nt(a, b):
    return lax.dot_general(a, b, (((1,), (1,)), ((), ())), preferred_element_type=F32)


def nn(a, b):
    return lax.dot_general(a, b, (((1,), (0,)), ((), ())), preferred_element_type=F32)


def tn(a, b):
    return lax.dot_general(a, b, (((0,), (0,)), ((), ())), preferred_element_type=F32)


def iota(shape, dim):
    return lax.broadcasted_iota(jnp.int32, shape, dim)


def sixth(v):
    return lax.shift_right_arithmetic(v * 43, 8)


def one(mask):
    return jnp.where(mask, 1.0, 0.0).astype(BF)


def take(ref, sem):
    pltpu.make_async_copy(ref, ref, sem).wait()


def kernel(
    x_ref, dy_ref, gv_ref, re_ref, rs_ref, sg_ref, su_ref, sd_ref, eg_ref, eu_ref, ed_ref,
    gx_ref, gg_ref, gsg_ref, gsu_ref, gsd_ref, neg_ref, neu_ref, ned_ref,
    tx, pb, pr, vcat, qm, qr, rall, qv, xf, df, wgu, dab, hq, pkb, s1, s2, s3, ret, back, rd,
    xs, xa, da, wsg, sp, r2, sdall, dxp, dxs, dxf, dxr, gp, arr, arl, fo,
    tok_send, tok_recv, tsib_send, tsib_recv, disp_send, disp_recv,
    ag_send, ag_recv, as_send, as_recv, y_send, y_recv, y2_send, y2_recv,
    ds_send, ds_recv, dx_send, dx_recv, rr_send, rr_recv, rl_send, rl_recv,
    br_send, br_recv, bl_send, bl_recv, c_send, c_recv, r_send, r_recv, b_send, b_recv,
):
    z = lax.axis_index("node")
    y = lax.axis_index("dp")
    l = lax.axis_index("local")
    x = l // 2
    c = l % 2
    oc = 1 - c

    def loc(xx, cc):
        return xx * 2 + cc

    bar = pltpu.get_barrier_semaphore()

    def greet(zz, ll, yy):
        pl.semaphore_signal(bar, inc=1, device_id=(zz, ll, yy), device_id_type=MESH)

    greet(z, loc(x, oc), y)

    def greet_plane(i, _):
        p = (x * 4 + y + 1 + i) % 16
        greet(z, loc(p // 4, c), p % 4)
        return 0

    lax.fori_loop(0, 15, greet_plane, 0)

    def greet_z(i, _):
        greet((z + 1 + i // 4) % 16, l, i % 4)
        return 0

    lax.fori_loop(0, 60, greet_z, 0)

    xv = x_ref[...].astype(F32)
    dv = dy_ref[...].astype(F32)
    even = jnp.concatenate([xv, dv[:, 256:320], dv[:, :256]], axis=1)
    odd = jnp.concatenate([xv[:, 64:320], dv[:, 0:64], xv[:, 0:64], dv[:, 64:320]], axis=1)
    is_even = c == 0
    tx[...] = jnp.where(is_even, even, odd).astype(BF)

    re = re_ref[...]
    rs = rs_ref[...]
    nd = lax.shift_right_arithmetic(re * 205, 11)
    ex = jnp.where(rs >= 0, lax.rem(nd + 16 - z, 16) * 4 + (re - nd * 10), -1)
    lane = iota((128, 128), 1)
    both = jnp.zeros((128, 128), F32)
    exf = ex.astype(F32)
    rsf = rs.astype(F32)
    gvf = gv_ref[...].astype(F32)
    for k in range(6):
        both = jnp.where(lane == k, exf[:, k : k + 1], both)
        both = jnp.where(lane == 8 + k, rsf[:, k : k + 1], both)
        vcat[k * 128 : (k + 1) * 128, :] = jnp.where(
            lane == rs[:, k : k + 1], gvf[:, k : k + 1], 0.0
        ).astype(BF)
    both_t = both.T
    e_t = both_t[0:8, :].astype(jnp.int32)
    s_t = both_t[8:16, :].astype(jnp.int32)
    p_t = jnp.where(e_t >= 0, e_t * 6 + s_t, -1)

    pl.semaphore_wait(bar, 76)

    for i in range(4):
        own = jnp.logical_and(x == i, y == x)

        @pl.when(own)
        def _():
            pltpu.make_async_copy(tx, xs.at[y, c], tok_recv.at[y]).start()

        @pl.when(jnp.logical_not(own))
        def _():
            pltpu.make_async_remote_copy(
                tx, xs.at[y, c], tok_send.at[i], tok_recv.at[y],
                device_id=(z, loc(i, c), x), device_id_type=MESH,
            ).start()

    row = iota((128, 128), 0)
    ry = lax.shift_right_arithmetic(row, 5)
    rr = row & 31
    rt = sixth(rr)
    rc = rr - rt * 6

    def chunk(i, _):
        k = i // 2
        h = i % 2
        dz = (8 - k) * (1 - h) + (8 + k) * ((k + 7) // 8) * h
        code = jnp.where(rr < 30, (dz * 4 + ry) * 6 + rc, -7)
        ecode = jnp.where(rr == 30, dz * 4 + ry, -7)
        hit = code == p_t[0:1, :]
        for kk in range(1, 6):
            hit = jnp.logical_or(hit, code == p_t[kk : kk + 1, :])
        prod = nn(one(hit), tx[...])
        out = nn(
            jnp.concatenate([one(ecode == e_t[kk : kk + 1, :]) for kk in range(6)], axis=1), vcat[...]
        )
        for t in range(5):
            out = out + jnp.where(rt == t, prod[:, t * 128 : (t + 1) * 128], 0.0)
        pb[dz] = out.astype(BF).reshape(4, 32, 128)
        for j in range(4):
            own = jnp.logical_and(dz == 0, y == j)

            @pl.when(own)
            def _():
                pltpu.make_async_copy(pb.at[dz, j], pr.at[dz, y], disp_recv.at[k]).start()

            @pl.when(jnp.logical_not(own))
            def _():
                pltpu.make_async_remote_copy(
                    pb.at[dz, j], pr.at[dz, y], disp_send, disp_recv.at[k],
                    device_id=((z + dz) % 16, l, j), device_id_type=MESH,
                ).start()
        return 0

    lax.fori_loop(0, 16, chunk, 0)

    col = iota((288, 256), 1)
    qrow = iota((288, 256), 0)
    cr = col & 31
    ct = sixth(cr)
    cb = lax.shift_right_arithmetic(col, 5) * 6
    dest = ct * 48 + cb + (cr - ct * 6)
    gate_row = qrow - 240 - cb
    qm[...] = one(
        jnp.logical_or(
            jnp.logical_and(cr < 30, qrow == dest),
            jnp.logical_and(cr == 30, jnp.logical_and(gate_row >= 0, gate_row < 6)),
        )
    )
    orow = iota((128, 240), 0)
    ocol = iota((128, 240), 1)
    og = lax.shift_right_arithmetic(orow, 4) * 6
    orr = orow & 15
    keep = jnp.logical_and(orr < 6, ocol == og + orr)
    keep = jnp.logical_or(keep, jnp.logical_and(jnp.logical_and(orr >= 6, orr < 12), ocol == 48 + og + orr - 6))
    tail = jnp.logical_and(orr >= 12, orr < 15)
    keep = jnp.logical_or(keep, jnp.logical_and(tail, ocol == 96 + og + orr - 12))
    keep = jnp.logical_or(keep, jnp.logical_and(tail, ocol == 144 + og + orr - 9))
    goff = ocol - 192 - og
    keep = jnp.logical_or(keep, jnp.logical_and(orr == 15, jnp.logical_and(goff >= 0, goff < 6)))
    qr[...] = one(keep)
    wgu[0:96, :] = eg_ref[0]
    wgu[96:192, :] = eu_ref[0]
    wsg[0:192, :] = sg_ref[...]
    wsg[192:384, :] = su_ref[...]

    lane48 = iota((48, 128), 1)
    row48 = iota((48, 128), 0)
    low48 = lane48 < 64
    c48 = row48 - sixth(row48) * 6

    for i in range(4):
        take(xs.at[i, c], tok_recv.at[i])
        pltpu.make_async_remote_copy(
            xs.at[i, c], xs.at[i, c], tsib_send.at[i], tsib_recv.at[i],
            device_id=(z, loc(x, oc), y), device_id_type=MESH,
        ).start()
    low128 = lane < 64
    for i in range(4):
        take(xs.at[i, oc], tsib_recv.at[i])
        te = xs[i, 0]
        to = xs[i, 1]
        te_t = te[:, 256:384].astype(F32)
        to_t = to[:, 256:384].astype(F32)
        rows = pl.ds(i * 128, 128)
        xa[rows, 0:256] = te[:, 0:256]
        xa[rows, 256:384] = jnp.where(low128, te_t, to_t).astype(BF)
        xa[rows, 384:640] = to[:, 0:256]
        da[rows, 0:256] = te[:, 384:640]
        da[rows, 256:384] = jnp.where(low128, pltpu.roll(te_t, 64, 1), pltpu.roll(to_t, 64, 1)).astype(BF)
        da[rows, 384:640] = to[:, 384:640]
    for i in range(4):
        rows = pl.ds(i * 128, 128)
        sp[i, :, 0:384] = nt(xa[rows, :], wsg[...]).astype(BF)
        sp[i, :, 384:576] = nt(da[rows, :], sd_ref[...]).astype(BF)
        sp[i, :, 576:640] = jnp.zeros((128, 64), BF)
    for o in range(1, 4):
        to_y = (y + o) % 4
        pltpu.make_async_remote_copy(
            sp.at[to_y], r2.at[y], y_send.at[o], y_recv.at[o],
            device_id=(z, l, to_y), device_id_type=MESH,
        ).start()
    r2[y] = sp[y]
    for o in range(1, 4):
        take(r2.at[(y + 4 - o) % 4], y_recv.at[o])
    tot = r2[0].astype(F32) + r2[1].astype(F32) + r2[2].astype(F32) + r2[3].astype(F32)
    sa = tot[:, 0:192]
    sb = tot[:, 192:384]
    se = tot[:, 384:576]
    sig = 1.0 / (1.0 + jnp.exp(-sa))
    sil = sa * sig
    sdall[y] = jnp.concatenate(
        [
            se * sb * sig * (1.0 + sa * (1.0 - sig)),
            se * sil,
            sil * sb,
            jnp.zeros((128, 64), F32),
        ],
        axis=1,
    ).astype(BF)
    for o in range(1, 4):
        pltpu.make_async_remote_copy(
            sdall.at[y], sdall.at[y], y2_send.at[o], y2_recv.at[o],
            device_id=(z, l, (y + o) % 4), device_id_type=MESH,
        ).start()
    for o in range(1, 4):
        take(sdall.at[(y + 4 - o) % 4], y2_recv.at[o])
    sall = sdall[...].reshape(512, 640)
    for t in range(5):
        cols = slice(t * 128, (t + 1) * 128)
        g2 = tn(sall[:, 0:384], xa[:, cols])
        g1 = tn(sall[:, 384:640], da[:, cols])
        gp[t * 3] = g2[0:192].astype(BF)
        gp[t * 3 + 1] = g2[192:384].astype(BF)
        gp[t * 3 + 2] = g1[0:192].astype(BF)
    gp[15] = jnp.zeros((192, 128), BF)

    zr = (z + 1) % 16
    zl = (z + 15) % 16

    def send_right(src, dst, ss, rsem):
        pltpu.make_async_remote_copy(
            src, dst, ss, rsem, device_id=(zr, l, y), device_id_type=MESH
        ).start()

    def send_left(src, dst, ss, rsem):
        pltpu.make_async_remote_copy(
            src, dst, ss, rsem, device_id=(zl, l, y), device_id_type=MESH
        ).start()

    def ring_sum(s):
        if s == 1:
            send_right(gp.at[(z + 8) % 16], arr.at[0], rr_send.at[0], rr_recv.at[0])
            send_left(gp.at[(z + 9) % 16], arl.at[0], rl_send.at[0], rl_recv.at[0])
            return
        if s <= 8:
            q = s - 2
            take(arr.at[q], rr_recv.at[q])
            arr[q] = (arr[q].astype(F32) + gp[(z + 9 - s) % 16].astype(F32)).astype(BF)
            send_right(arr.at[q], arr.at[q + 1], rr_send.at[q + 1], rr_recv.at[q + 1])
            if s <= 7:
                take(arl.at[q], rl_recv.at[q])
                arl[q] = (arl[q].astype(F32) + gp[(z + 8 + s) % 16].astype(F32)).astype(BF)
                send_left(arl.at[q], arl.at[q + 1], rl_send.at[q + 1], rl_recv.at[q + 1])
            return
        if s == 9:
            take(arr.at[7], rr_recv.at[7])
            take(arl.at[6], rl_recv.at[6])
            fo[z] = (gp[z].astype(F32) + arr[7].astype(F32) + arl[6].astype(F32)).astype(BF)
        q = s - 9
        if q > 0 and q <= 8:
            take(fo.at[(z + 16 - q) % 16], br_recv.at[q - 1])
        if q > 0 and q <= 7:
            take(fo.at[(z + q) % 16], bl_recv.at[q - 1])
        if q < 8:
            src = fo.at[(z + 16 - q) % 16]
            send_right(src, src, br_send.at[q], br_recv.at[q])
        if q < 7:
            src = fo.at[(z + q) % 16]
            send_left(src, src, bl_send.at[q], bl_recv.at[q])

    ring_sum(1)

    for i in range(4):
        part = nn(sall[i * 128 : (i + 1) * 128, 0:384], wsg[...]).astype(BF)
        dxp[0, i] = part[:, 0:384]
        dxp[1, i] = part[:, 256:640]
    dx_sib = pltpu.make_async_remote_copy(
        dxp.at[oc], dxs, ds_send, ds_recv, device_id=(z, loc(x, oc), y), device_id_type=MESH
    )
    dx_sib.start()

    ring_sum(2)

    def unpack(k):
        a = 8 - k
        b = (8 + k) % 16 if k else 0
        take(pr.at[0:2], disp_recv.at[k])
        u = nn(qm[...], jnp.concatenate([pr[a].reshape(128, 128), pr[b].reshape(128, 128)], axis=0))
        for t in range(5):
            rall[x, c, k, :, t * 128 : (t + 1) * 128] = u[t * 48 : (t + 1) * 48].astype(BF)
        q = jnp.sum(jnp.where(lane48 == c48, u[240:288], 0.0), axis=1, keepdims=True)
        qv[k * 48 : (k + 1) * 48, :] = jnp.broadcast_to(q, (48, 128))
        blk = rall.at[x, c, k]
        for n, dx in enumerate((1, 3)):
            pltpu.make_async_remote_copy(
                blk, blk, ag_send.at[k, n], ag_recv.at[k, n],
                device_id=(z, loc((x + dx) % 4, c), y), device_id_type=MESH,
            ).start()
        pltpu.make_async_remote_copy(
            blk, blk, as_send.at[k, 0], as_recv.at[k, 0],
            device_id=(z, loc(x, oc), y), device_id_type=MESH,
        ).start()

    def to_sib(blk, k, n):
        pltpu.make_async_remote_copy(
            blk, blk, as_send.at[k, n], as_recv.at[k, n],
            device_id=(z, loc(x, oc), y), device_id_type=MESH,
        ).start()

    def forward(k):
        left = rall.at[(x + 3) % 4, c, k]
        right = rall.at[(x + 1) % 4, c, k]
        take(left, ag_recv.at[k, 0])
        if k % 2 == 0:
            pltpu.make_async_remote_copy(
                left, left, ag_send.at[k, 2], ag_recv.at[k, 2],
                device_id=(z, loc((x + 1) % 4, c), y), device_id_type=MESH,
            ).start()
        to_sib(left, k, 1)
        take(right, ag_recv.at[k, 1])
        if k % 2 == 1:
            pltpu.make_async_remote_copy(
                right, right, ag_send.at[k, 2], ag_recv.at[k, 2],
                device_id=(z, loc((x + 3) % 4, c), y), device_id_type=MESH,
            ).start()
        to_sib(right, k, 2)

    def across(k):
        far = rall.at[(x + 2) % 4, c, k]
        take(far, ag_recv.at[k, 2])
        to_sib(far, k, 3)

    def settle(k):
        for n, dx in enumerate((0, 3, 1, 2)):
            take(rall.at[(x + dx) % 4, oc, k], as_recv.at[k, n])

    def half(h):
        lo = 192 * h
        rows = slice(lo, lo + 192)
        lane192 = iota((192, 128), 1) < 64
        for p in range(4):
            te = rall[p, 0, 4 * h : 4 * h + 4].reshape(192, 640)
            to = rall[p, 1, 4 * h : 4 * h + 4].reshape(192, 640)
            te_t = te[:, 256:384].astype(F32)
            to_t = to[:, 256:384].astype(F32)
            b = p * 640
            xf[rows, b : b + 256] = te[:, 0:256]
            xf[rows, b + 256 : b + 384] = jnp.where(lane192, te_t, to_t).astype(BF)
            xf[rows, b + 384 : b + 640] = to[:, 0:256]
            df[rows, b : b + 256] = te[:, 384:640]
            df[rows, b + 256 : b + 384] = jnp.where(
                lane192, pltpu.roll(te_t, 64, 1), pltpu.roll(to_t, 64, 1)
            ).astype(BF)
            df[rows, b + 384 : b + 640] = to[:, 384:640]
        ab = nt(xf[rows, :], wgu[...])
        e = nt(df[rows, :], ed_ref[0])
        a = ab[:, 0:96]
        b = ab[:, 96:192]
        sg = 1.0 / (1.0 + jnp.exp(-a))
        sl = a * sg
        hid = sl * b
        gpart = jnp.sum(e * hid, axis=1, keepdims=True)
        q = qv[rows, 0:1]
        qe = q * e
        dab[rows, :] = jnp.concatenate([qe * b * sg * (1.0 + a * (1.0 - sg)), qe * sl], axis=1).astype(BF)
        hq[rows, :] = (q * hid).astype(BF)
        rd[...] = nn(dab[rows, :], wgu[...]).astype(BF)
        for k in range(4):
            r48 = slice(k * 48, (k + 1) * 48)
            g = jnp.where(lane48 == c48, gpart[r48], 0.0).astype(BF)
            zero = jnp.zeros((48, 128), F32)
            cols = []
            for p in range(4):
                t = rd[r48, p * 640 + 256 : p * 640 + 384].astype(F32)
                u = pltpu.roll(t, 64, 1)
                for cc in range(2):
                    b = p * 640 + cc * 384
                    first, second = (t, u) if cc == 0 else (u, t)
                    cols.append(
                        jnp.concatenate(
                            [
                                rd[r48, b : b + 128],
                                rd[r48, b + 128 : b + 256],
                                jnp.where(low48, first, zero).astype(BF),
                                jnp.where(low48, zero, second).astype(BF),
                                g,
                            ],
                            axis=0,
                        )
                    )
            packed = nn(qr[...], jnp.concatenate(cols, axis=1)).astype(BF)
            for ll in range(8):
                pkb[h, ll, k] = packed[:, ll * 128 : (ll + 1) * 128]
        for o in (2, 1, 3, 0):
            xx = (x + o) % 4
            pltpu.make_async_remote_copy(
                pkb.at[h, loc(xx, oc)], s1.at[h, xx], c_send.at[h, o], c_recv.at[h, o],
                device_id=(z, loc(x, oc), y), device_id_type=MESH,
            ).start()

    def reduce_pair(h):
        for o in (2, 1, 3, 0):
            xx = (x + o) % 4
            take(s1.at[h, xx], c_recv.at[h, o])
            v = (pkb[h, loc(xx, c)].astype(F32) + s1[h, xx].astype(F32)).astype(BF)
            if o == 0:
                s3[h, x] = v
            else:
                s2[h, xx] = v
                pltpu.make_async_remote_copy(
                    s2.at[h, xx], s3.at[h, x], r_send.at[h, o], r_recv.at[h, o],
                    device_id=(z, loc(xx, c), y), device_id_type=MESH,
                ).start()

    def give_back(h):
        for o in (1, 2, 3):
            take(s3.at[h, (x + 4 - o) % 4], r_recv.at[h, o])
        for k in range(4):
            v = s3[h, 0, k].astype(F32) + s3[h, 1, k].astype(F32)
            v = v + s3[h, 2, k].astype(F32) + s3[h, 3, k].astype(F32)
            ret[h, k] = v.astype(BF).reshape(8, 16, 128)
            kk = 4 * h + k
            for n, dz in enumerate((8 - kk, (8 + kk) % 16 if kk else 0)):
                for j in range(4):
                    src = ret.at[h, k, n * 4 + j]
                    dst = back.at[dz, y]
                    if dz == 0:

                        @pl.when(y == j)
                        def _():
                            pltpu.make_async_copy(src, dst, b_recv).start()

                        @pl.when(y != j)
                        def _():
                            pltpu.make_async_remote_copy(
                                src, dst, b_send, b_recv, device_id=(z, l, j), device_id_type=MESH
                            ).start()

                    else:
                        pltpu.make_async_remote_copy(
                            src, dst, b_send, b_recv,
                            device_id=((z + 16 - dz) % 16, l, j), device_id_type=MESH,
                        ).start()

    def dx_out():
        dx_sib.wait_recv()
        for i in range(4):
            own = jnp.logical_and(x == y, y == i)
            dxf[i] = (dxp[c, i].astype(F32) + dxs[i].astype(F32)).astype(BF)

            @pl.when(own)
            def _():
                pltpu.make_async_copy(dxf.at[i], dxr.at[x], dx_recv.at[x]).start()

            @pl.when(jnp.logical_not(own))
            def _():
                pltpu.make_async_remote_copy(
                    dxf.at[i], dxr.at[x], dx_send.at[i], dx_recv.at[x],
                    device_id=(z, loc(y, c), i), device_id_type=MESH,
                ).start()

    for k in range(4):
        unpack(k)
        if k >= 1:
            forward(k - 1)
        if k >= 2:
            across(k - 2)
    ring_sum(3)
    for k in range(4, 8):
        unpack(k)
        forward(k - 1)
        across(k - 2)
        if k % 2:
            ring_sum(4 + (k - 5) // 2)
    for k in range(4):
        settle(k)
    half(0)
    ring_sum(6)
    forward(7)
    across(6)
    reduce_pair(0)
    across(7)
    ring_sum(7)
    for k in range(4, 8):
        settle(k)
    half(1)
    ring_sum(8)
    give_back(0)
    reduce_pair(1)
    ring_sum(9)
    dx_out()
    ring_sum(10)
    give_back(1)

    def weight_grads(i, _):
        cols = pl.ds(pl.multiple_of(i * 640, 128), 640)
        g2 = tn(dab[...], xf[:, cols])
        neg_ref[0, :, cols] = g2[0:96].astype(BF)
        neu_ref[0, :, cols] = g2[96:192].astype(BF)
        ned_ref[0, :, cols] = tn(hq[...], df[:, cols]).astype(BF)
        return 0

    lax.fori_loop(0, 2, weight_grads, 0)
    ring_sum(11)
    lax.fori_loop(2, 4, weight_grads, 0)
    ring_sum(12)

    jc = iota((128, 1024), 1)
    jr = jc & 15
    jg = lax.shift_right_arithmetic(jc, 4) * 6
    cls_a = jr < 6
    cls_b = jnp.logical_and(jr >= 6, jr < 12)
    cls_t = jnp.logical_and(jr >= 12, jr < 15)
    code = jg + jnp.where(cls_a, jr, jnp.where(cls_b, jr - 6, jr - 12))
    pos = jnp.where(rs >= 0, ex * 6 + rs, -100)
    hit = code == pos[:, 0:1]
    hit2 = code + 3 == pos[:, 0:1]
    for kk in range(1, 6):
        hit = jnp.logical_or(hit, code == pos[:, kk : kk + 1])
        hit2 = jnp.logical_or(hit2, code + 3 == pos[:, kk : kk + 1])
    sel = jnp.concatenate(
        [
            one(jnp.logical_and(hit, cls_a)),
            one(jnp.logical_and(hit, cls_b)),
            one(jnp.logical_and(hit, cls_t)),
            one(jnp.logical_and(hit2, cls_t)),
        ],
        axis=0,
    )
    grow = one(jnp.logical_and(iota((64, 1024), 1) == iota((64, 1024), 0) * 16 + 15, True))
    ring_sum(13)

    take(back, b_recv)
    rows = back[...].reshape(1024, 128)
    got = nn(sel, rows)
    gates = nn(grow, rows).astype(BF)
    lane64 = iota((128, 64), 1)
    acc = jnp.zeros((128, 128), F32)
    for kk in range(6):
        gk = nn(one(lane64 == ex[:, kk : kk + 1]), gates)
        gk = jnp.sum(jnp.where(lane == rs[:, kk : kk + 1], gk, 0.0), axis=1, keepdims=True)
        acc = jnp.where(lane == kk, gk, acc)
    gg_ref[...] = acc[:, 0:6]
    ring_sum(14)
    for i in range(4):
        take(dxr.at[i], dx_recv.at[i])
    m = dxr[0].astype(F32) + dxr[1].astype(F32) + dxr[2].astype(F32) + dxr[3].astype(F32)
    tl = got[256:384, 0:64] + got[384:512, 64:128]
    evn = jnp.concatenate([m[:, 0:128] + got[0:128], m[:, 128:256] + got[128:256], m[:, 256:320] + tl], axis=1)
    od = jnp.concatenate([m[:, 64:128] + tl, m[:, 128:256] + got[0:128], m[:, 256:384] + got[128:256]], axis=1)
    gx_ref[...] = jnp.where(is_even, evn, od).astype(BF)

    ring_sum(15)
    ring_sum(16)
    ring_sum(17)
    for t in range(5):
        cols = slice(t * 128, (t + 1) * 128)
        gsg_ref[:, cols] = fo[t * 3]
        gsu_ref[:, cols] = fo[t * 3 + 1]
        gsd_ref[:, cols] = fo[t * 3 + 2]

    for i in range(4):
        own = jnp.logical_and(x == i, y == x)

        @pl.when(jnp.logical_not(own))
        def _():
            take(tx, tok_send.at[i])

        take(xs.at[i, c], tsib_send.at[i])
        own2 = jnp.logical_and(x == y, y == i)

        @pl.when(jnp.logical_not(own2))
        def _():
            take(dxf.at[i], dx_send.at[i])

    pbf = pb.reshape(64, 32, 128)
    take(pbf.at[0:63], disp_send)
    backf = back.reshape(64, 16, 128)
    take(backf.at[0:63], b_send)
    for o in range(1, 4):
        take(sp.at[0], y_send.at[o])
        take(sdall.at[0], y2_send.at[o])
    dx_sib.wait_send()
    for k in range(8):
        for n in range(3):
            take(rall.at[0, 0, k], ag_send.at[k, n])
        for n in range(4):
            take(rall.at[0, 0, k], as_send.at[k, n])
    for h in range(2):
        for o in range(4):
            take(s1.at[h, 0], c_send.at[h, o])
        for o in range(1, 4):
            take(s2.at[h, 0], r_send.at[h, o])
    for q in range(8):
        take(arr.at[0], rr_send.at[q])
        take(fo.at[0], br_send.at[q])
    for q in range(7):
        take(arl.at[0], rl_send.at[q])
        take(fo.at[0], bl_send.at[q])


def on_device(*args):
    sem = pltpu.SemaphoreType.DMA
    vm = pltpu.VMEM
    out_shape = (
        jax.ShapeDtypeStruct((128, 320), BF),
        jax.ShapeDtypeStruct((128, 6), F32),
        jax.ShapeDtypeStruct((192, 640), BF),
        jax.ShapeDtypeStruct((192, 640), BF),
        jax.ShapeDtypeStruct((192, 640), BF),
        jax.ShapeDtypeStruct((1, 96, 2560), BF),
        jax.ShapeDtypeStruct((1, 96, 2560), BF),
        jax.ShapeDtypeStruct((1, 96, 2560), BF),
    )
    scratch = [
        vm((128, 640), BF),
        vm((16, 4, 32, 128), BF),
        vm((16, 4, 32, 128), BF),
        vm((768, 128), BF),
        vm((288, 256), BF),
        vm((128, 240), BF),
        vm((4, 2, 8, 48, 640), BF),
        vm((384, 128), F32),
        vm((384, 2560), BF),
        vm((384, 2560), BF),
        vm((192, 2560), BF),
        vm((384, 192), BF),
        vm((384, 96), BF),
        vm((2, 8, 4, 128, 128), BF),
        vm((2, 4, 4, 128, 128), BF),
        vm((2, 4, 4, 128, 128), BF),
        vm((2, 4, 4, 128, 128), BF),
        vm((2, 4, 8, 16, 128), BF),
        vm((16, 4, 16, 128), BF),
        vm((192, 2560), BF),
        vm((4, 2, 128, 640), BF),
        vm((512, 640), BF),
        vm((512, 640), BF),
        vm((384, 640), BF),
        vm((4, 128, 640), BF),
        vm((4, 128, 640), BF),
        vm((4, 128, 640), BF),
        vm((2, 4, 128, 384), BF),
        vm((4, 128, 384), BF),
        vm((4, 128, 384), BF),
        vm((4, 128, 384), BF),
        vm((16, 192, 128), BF),
        vm((8, 192, 128), BF),
        vm((7, 192, 128), BF),
        vm((16, 192, 128), BF),
        sem((4,)), sem((4,)), sem((4,)), sem((4,)), sem, sem((8,)),
        sem((8, 3)), sem((8, 3)), sem((8, 4)), sem((8, 4)),
        sem((4,)), sem((4,)), sem((4,)), sem((4,)),
        sem, sem, sem((4,)), sem((4,)),
        sem((8,)), sem((8,)), sem((7,)), sem((7,)),
        sem((8,)), sem((8,)), sem((7,)), sem((7,)),
        sem((2, 4)), sem((2, 4)), sem((2, 4)), sem((2, 4)), sem, sem,
    ]
    return pl.pallas_call(
        kernel,
        out_shape=out_shape,
        in_specs=[pl.BlockSpec(memory_space=pltpu.VMEM)] * 11,
        out_specs=tuple([pl.BlockSpec(memory_space=pltpu.VMEM)] * 8),
        scratch_shapes=scratch,
        compiler_params=pltpu.CompilerParams(
            collective_id=0, has_side_effects=True, vmem_limit_bytes=56 * 1024 * 1024
        ),
        cost_estimate=pl.CostEstimate(flops=3_000_000_000, bytes_accessed=6_000_000, transcendentals=100_000),
    )(*args)


def solution(mesh):
    in_specs = (
        P(("node", "dp"), "local"),
        P(("node", "dp"), "local"),
        P(("node", "dp"), None),
        P(("node", "dp"), None),
        P(("node", "dp"), None),
        P("local", "dp"),
        P("local", "dp"),
        P("local", "dp"),
        P(("node", "dp"), "local", None),
        P(("node", "dp"), "local", None),
        P(("node", "dp"), "local", None),
    )
    out_specs = (
        P(("node", "dp"), "local"),
        P(("node", "dp"), None),
        P("local", "dp"),
        P("local", "dp"),
        P("local", "dp"),
        P(("node", "dp"), "local", None),
        P(("node", "dp"), "local", None),
        P(("node", "dp"), "local", None),
    )
    return jax.shard_map(
        on_device, mesh=mesh, in_specs=in_specs, out_specs=out_specs, check_vma=False
    )
```

time: 595 us -> 153 us (0.26)
  waiting for transfers between devices: 313 us -> 0 us
  Pallas kernels: 0 us -> 138 us
  blocking collectives: 138 us -> 0 us
  starting transfers between devices: 56.6 us -> 0 us
  local copies, waits for them, and re-layouts: 41.1 us -> 13.4 us
  matrix products: 26.2 us -> 0 us
  between operations: 14.2 us -> 0.68 us
    all_to_all x7 -> x0, waiting for transfers between devices: 197 us -> none  [the longest x1 104 us: on_device(): lax.all_to_all(send_x.reshape(groups, CAP, row_width), ('node', 'dp'), sp...]
    pallas_call x0 -> x1, Pallas kernels: none -> 138 us  [on_device(): pl.pallas_call(kernel, out_shape=out_shape, in_specs=[pl.BlockSpec(memory...]
    all_gather x7 -> x0, blocking collectives: 116 us -> none  [the longest x1 17.9 us: on_device(): lax.all_gather(shared_gate, 'dp', axis=1, tiled=True)]
    psum x1 -> x0, waiting for transfers between devices: 116 us -> none  [on_device(): lax.psum(sum_gate.astype(jnp.bfloat16), 'node').astype(jnp.float32)]
    all_to_all x7 -> x0, starting transfers between devices: 56.4 us -> none  [the longest x1 16 us: on_device(): lax.all_to_all(send_x.reshape(groups, CAP, row_width), ('node', 'dp'), sp...]
    dot_general x19 -> x0, matrix products: 26.2 us -> none  [the longest x6 6.06 us: contract_rows(): lax.dot_general(left, right, (((0,), (0,)), ((), ())), preferred_element_...]
    psum x1 -> x0, blocking collectives: 21.3 us -> none  [on_device(): gate_grad = lax.psum(gate_part, 'local')]
    reshape x6 -> x0, local copies, waits for them, and re-layouts: 16.1 us -> none  [the longest x1 4.16 us: on_device(): rows_dy = recv_dy.reshape(slot_count, model_width)]
  transfers between devices with their start and end apart: 12 -> 0, of which waited for: 6 -> 0; matrix products, arithmetic and copies ran while one was open for 9% -> 0% of each run, Pallas kernels for 0% -> 0%
where the time goes in v1:
time: 153 us; the launch traced here: 152 us
  Pallas kernels  138 us (90%)
  local copies, waits for them, and re-layouts  13.4 us (9%)
    pallas_call x1, Pallas kernels, on_device(): pl.pallas_call(kernel, out_shape=out_shape, in_specs=[pl.BlockSpec(memory...  138 us
    unnamed x31, local copies, waits for them, and re-layouts  10.2 us
    pallas_call x2, local copies, waits for them, and re-layouts, on_device(): pl.pallas_call(kernel, out_shape=out_shape, in_specs=[pl.BlockSpec(memory...  3.18 us

profile of v1, /device:TPU:6, one launch (start us, length us, event | category | flops | bytes accessed | tf_op | source)
XLA Modules:
  0.0 152.2 jit_solution(1105483589396313558)
XLA Ops:
  0.6 0.0 copy-start.8
  0.6 0.0 copy-start.6
  0.7 1.4 copy.21.gv_ref
  2.1 0.0 copy-done.8
  2.1 0.0 copy-start.9
  2.1 0.7 copy.22.re_ref
  2.8 0.0 copy-done.9
  2.8 0.7 copy.23.rs_ref
  3.6 0.0 copy-done.6
  3.6 0.0 copy-start.7
  3.6 0.8 copy.19.x_ref
  4.3 0.1 copy-done.7
  4.5 0.8 copy.20.dy_ref
  5.2 138.1 %shard_map.170 = (bf16[128,320]{1,0:T(8,128)(2,1)}, f32[128,6]{1,0:T(8,128)}, bf16[192,640]{1,0:T(8,128)(2,1)}, bf16[192,640]{1,0:T(8,128)(2,1)}, bf16[192,640]{...) custom-call(bf16[128,320]{1,0:T(8,128)(2,1)} %copy.19.x_ref, ...), custom_call_target="tpu_custom_call" | custom-call | flops 3000000000 | bytes 6000000 | tf_op jit(solution)/shard_map/pallas_call | solution.py:696
  143.4 0.0 copy-start.5
  143.4 1.7 %copy.24 = bf16[128,320]{0,1:T(8,128)(2,1)} copy(bf16[128,320]{1,0:T(8,128)(2,1)} %get-tuple-element.8) | data formatting | bytes 163840 | tf_op jit(solution)/shard_map/pallas_call | solution.py:696
  145.0 1.5 copy.25
  146.5 0.0 copy-done.5
  146.6 0.0 copy-start.4
  146.6 0.0 copy-start.3
  146.6 0.7 copy.32
  147.2 0.3 copy-done.4
  147.6 0.0 copy-start.2
  147.6 0.7 copy.33
  148.3 0.0 copy-done.3
  148.3 0.7 copy.34
  149.0 0.0 copy-done.2
  149.0 0.8 copy.35
  149.8 0.4 copy-done.1
  150.2 0.8 copy.36
  151.0 0.4 copy-done
  151.4 0.8 copy.37
  (2 shorter events, 0.0 us)
Async XLA Ops:
  0.6 1.5 copy-start.8
  0.6 2.9 %copy-start.6 = (bf16[128,320]{0,1:T(8,128)(2,1)S(1)}, bf16[128,320]{0,1:T(8,128)(2,1)}, u32[]{:S(2)}) copy-start(bf16[128,320]{0,1:T(8,128)(2,1)} %param.11) | copy-start | bytes 245764
  2.1 0.7 copy-start.9
  3.6 0.9 copy-start.7
  143.4 3.2 %copy-start.5 = (bf16[192,640]{1,0:T(8,128)(2,1)S(1)}, bf16[192,640]{1,0:T(8,128)(2,1)}, u32[]{:S(2)}) copy-start(bf16[192,640]{1,0:T(8,128)(2,1)} %get-tuple-element.26) | copy-start | bytes 737284
  146.6 1.0 copy-start.4
  146.6 1.7 %copy-start.3 = (bf16[192,640]{1,0:T(8,128)(2,1)S(1)}, bf16[192,640]{1,0:T(8,128)(2,1)}, u32[]{:S(2)}) copy-start(bf16[192,640]{1,0:T(8,128)(2,1)} %get-tuple-element.28) | copy-start | bytes 737284
  147.6 1.4 copy-start.2
  149.0 1.2 copy-start.1
  150.2 1.2 copy-start

commit v2 on v1

--- a/solution.py
+++ b/solution.py
@@ -42,7 +42,7 @@
     x_ref, dy_ref, gv_ref, re_ref, rs_ref, sg_ref, su_ref, sd_ref, eg_ref, eu_ref, ed_ref,
     gx_ref, gg_ref, gsg_ref, gsu_ref, gsd_ref, neg_ref, neu_ref, ned_ref,
     tx, pb, pr, vcat, qm, qr, rall, qv, xf, df, wgu, dab, hq, pkb, s1, s2, s3, ret, back, rd,
-    xs, xa, da, wsg, sp, r2, sdall, dxp, dxs, dxf, dxr, gp, arr, arl, fo,
+    xs, xa, da, wsg, sp, r2, sdall, dxp, dxs, dxf, dxr, gp, arr, arl, fo, selm,
     tok_send, tok_recv, tsib_send, tsib_recv, disp_send, disp_recv,
     ag_send, ag_recv, as_send, as_recv, y_send, y_recv, y2_send, y2_recv,
     ds_send, ds_recv, dx_send, dx_recv, rr_send, rr_recv, rl_send, rl_recv,
@@ -78,32 +78,37 @@
 
     lax.fori_loop(0, 60, greet_z, 0)
 
-    xv = x_ref[...].astype(F32)
-    dv = dy_ref[...].astype(F32)
+    lane = iota((128, 128), 1)
+    row = iota((128, 128), 0)
+    eye = one(lane == row)
+    xv = nt(eye, x_ref[...])
+    dv = nt(eye, dy_ref[...])
     even = jnp.concatenate([xv, dv[:, 256:320], dv[:, :256]], axis=1)
     odd = jnp.concatenate([xv[:, 64:320], dv[:, 0:64], xv[:, 0:64], dv[:, 64:320]], axis=1)
     is_even = c == 0
     tx[...] = jnp.where(is_even, even, odd).astype(BF)
 
-    re = re_ref[...]
-    rs = rs_ref[...]
-    nd = lax.shift_right_arithmetic(re * 205, 11)
-    ex = jnp.where(rs >= 0, lax.rem(nd + 16 - z, 16) * 4 + (re - nd * 10), -1)
-    lane = iota((128, 128), 1)
+    re_t = re_ref[...]
+    rs_t = rs_ref[...]
+    nd = lax.shift_right_arithmetic(re_t * 205, 11)
+    e_t = jnp.where(rs_t >= 0, lax.rem(nd + 16 - z, 16) * 4 + (re_t - nd * 10), -1)
+    p_t = jnp.where(rs_t >= 0, e_t * 6 + rs_t, -1)
+    e_f = e_t.astype(F32)
+    s_f = rs_t.astype(F32)
+    g_f = gv_ref[...].astype(F32)
     both = jnp.zeros((128, 128), F32)
-    exf = ex.astype(F32)
-    rsf = rs.astype(F32)
-    gvf = gv_ref[...].astype(F32)
     for k in range(6):
-        both = jnp.where(lane == k, exf[:, k : k + 1], both)
-        both = jnp.where(lane == 8 + k, rsf[:, k : k + 1], both)
+        both = jnp.where(row == k, e_f[k : k + 1, :], both)
+        both = jnp.where(row == 8 + k, s_f[k : k + 1, :], both)
+        both = jnp.where(row == 16 + k, g_f[k : k + 1, :], both)
+    turned = both.T
+    turned_i = turned.astype(jnp.int32)
+    ex = turned_i[:, 0:6]
+    rs = turned_i[:, 8:14]
+    for k in range(6):
         vcat[k * 128 : (k + 1) * 128, :] = jnp.where(
-            lane == rs[:, k : k + 1], gvf[:, k : k + 1], 0.0
+            lane == rs[:, k : k + 1], turned[:, 16 + k : 17 + k], 0.0
         ).astype(BF)
-    both_t = both.T
-    e_t = both_t[0:8, :].astype(jnp.int32)
-    s_t = both_t[8:16, :].astype(jnp.int32)
-    p_t = jnp.where(e_t >= 0, e_t * 6 + s_t, -1)
 
     pl.semaphore_wait(bar, 76)
 
@@ -121,7 +126,6 @@
                 device_id=(z, loc(i, c), x), device_id_type=MESH,
             ).start()
 
-    row = iota((128, 128), 0)
     ry = lax.shift_right_arithmetic(row, 5)
     rr = row & 31
     rt = sixth(rr)
@@ -195,72 +199,6 @@
     low48 = lane48 < 64
     c48 = row48 - sixth(row48) * 6
 
-    for i in range(4):
-        take(xs.at[i, c], tok_recv.at[i])
-        pltpu.make_async_remote_copy(
-            xs.at[i, c], xs.at[i, c], tsib_send.at[i], tsib_recv.at[i],
-            device_id=(z, loc(x, oc), y), device_id_type=MESH,
-        ).start()
-    low128 = lane < 64
-    for i in range(4):
-        take(xs.at[i, oc], tsib_recv.at[i])
-        te = xs[i, 0]
-        to = xs[i, 1]
-        te_t = te[:, 256:384].astype(F32)
-        to_t = to[:, 256:384].astype(F32)
-        rows = pl.ds(i * 128, 128)
-        xa[rows, 0:256] = te[:, 0:256]
-        xa[rows, 256:384] = jnp.where(low128, te_t, to_t).astype(BF)
-        xa[rows, 384:640] = to[:, 0:256]
-        da[rows, 0:256] = te[:, 384:640]
-        da[rows, 256:384] = jnp.where(low128, pltpu.roll(te_t, 64, 1), pltpu.roll(to_t, 64, 1)).astype(BF)
-        da[rows, 384:640] = to[:, 384:640]
-    for i in range(4):
-        rows = pl.ds(i * 128, 128)
-        sp[i, :, 0:384] = nt(xa[rows, :], wsg[...]).astype(BF)
-        sp[i, :, 384:576] = nt(da[rows, :], sd_ref[...]).astype(BF)
-        sp[i, :, 576:640] = jnp.zeros((128, 64), BF)
-    for o in range(1, 4):
-        to_y = (y + o) % 4
-        pltpu.make_async_remote_copy(
-            sp.at[to_y], r2.at[y], y_send.at[o], y_recv.at[o],
-            device_id=(z, l, to_y), device_id_type=MESH,
-        ).start()
-    r2[y] = sp[y]
-    for o in range(1, 4):
-        take(r2.at[(y + 4 - o) % 4], y_recv.at[o])
-    tot = r2[0].astype(F32) + r2[1].astype(F32) + r2[2].astype(F32) + r2[3].astype(F32)
-    sa = tot[:, 0:192]
-    sb = tot[:, 192:384]
-    se = tot[:, 384:576]
-    sig = 1.0 / (1.0 + jnp.exp(-sa))
-    sil = sa * sig
-    sdall[y] = jnp.concatenate(
-        [
-            se * sb * sig * (1.0 + sa * (1.0 - sig)),
-            se * sil,
-            sil * sb,
-            jnp.zeros((128, 64), F32),
-        ],
-        axis=1,
-    ).astype(BF)
-    for o in range(1, 4):
-        pltpu.make_async_remote_copy(
-            sdall.at[y], sdall.at[y], y2_send.at[o], y2_recv.at[o],
-            device_id=(z, l, (y + o) % 4), device_id_type=MESH,
-        ).start()
-    for o in range(1, 4):
-        take(sdall.at[(y + 4 - o) % 4], y2_recv.at[o])
-    sall = sdall[...].reshape(512, 640)
-    for t in range(5):
-        cols = slice(t * 128, (t + 1) * 128)
-        g2 = tn(sall[:, 0:384], xa[:, cols])
-        g1 = tn(sall[:, 384:640], da[:, cols])
-        gp[t * 3] = g2[0:192].astype(BF)
-        gp[t * 3 + 1] = g2[192:384].astype(BF)
-        gp[t * 3 + 2] = g1[0:192].astype(BF)
-    gp[15] = jnp.zeros((192, 128), BF)
-
     zr = (z + 1) % 16
     zl = (z + 15) % 16
 
@@ -275,48 +213,39 @@
         ).start()
 
     def ring_sum(s):
+        for u in range(2):
+            ring_part(s, u, pl.ds(u * 96, 96))
+
+    def ring_part(s, u, w):
         if s == 1:
-            send_right(gp.at[(z + 8) % 16], arr.at[0], rr_send.at[0], rr_recv.at[0])
-            send_left(gp.at[(z + 9) % 16], arl.at[0], rl_send.at[0], rl_recv.at[0])
+            send_right(gp.at[(z + 8) % 16, w], arr.at[0, w], rr_send.at[0, u], rr_recv.at[0, u])
+            send_left(gp.at[(z + 9) % 16, w], arl.at[0, w], rl_send.at[0, u], rl_recv.at[0, u])
             return
         if s <= 8:
             q = s - 2
-            take(arr.at[q], rr_recv.at[q])
-            arr[q] = (arr[q].astype(F32) + gp[(z + 9 - s) % 16].astype(F32)).astype(BF)
-            send_right(arr.at[q], arr.at[q + 1], rr_send.at[q + 1], rr_recv.at[q + 1])
+            take(arr.at[q, w], rr_recv.at[q, u])
+            arr[q, w] = (arr[q, w].astype(F32) + gp[(z + 9 - s) % 16, w].astype(F32)).astype(BF)
+            send_right(arr.at[q, w], arr.at[q + 1, w], rr_send.at[q + 1, u], rr_recv.at[q + 1, u])
             if s <= 7:
-                take(arl.at[q], rl_recv.at[q])
-                arl[q] = (arl[q].astype(F32) + gp[(z + 8 + s) % 16].astype(F32)).astype(BF)
-                send_left(arl.at[q], arl.at[q + 1], rl_send.at[q + 1], rl_recv.at[q + 1])
+                take(arl.at[q, w], rl_recv.at[q, u])
+                arl[q, w] = (arl[q, w].astype(F32) + gp[(z + 8 + s) % 16, w].astype(F32)).astype(BF)
+                send_left(arl.at[q, w], arl.at[q + 1, w], rl_send.at[q + 1, u], rl_recv.at[q + 1, u])
             return
         if s == 9:
-            take(arr.at[7], rr_recv.at[7])
-            take(arl.at[6], rl_recv.at[6])
-            fo[z] = (gp[z].astype(F32) + arr[7].astype(F32) + arl[6].astype(F32)).astype(BF)
+            take(arr.at[7, w], rr_recv.at[7, u])
+            take(arl.at[6, w], rl_recv.at[6, u])
+            fo[z, w] = (gp[z, w].astype(F32) + arr[7, w].astype(F32) + arl[6, w].astype(F32)).astype(BF)
         q = s - 9
         if q > 0 and q <= 8:
-            take(fo.at[(z + 16 - q) % 16], br_recv.at[q - 1])
+            take(fo.at[(z + 16 - q) % 16, w], br_recv.at[q - 1, u])
+        if q < 8:
+            src = fo.at[(z + 16 - q) % 16, w]
+            send_right(src, src, br_send.at[q, u], br_recv.at[q, u])
         if q > 0 and q <= 7:
-            take(fo.at[(z + q) % 16], bl_recv.at[q - 1])
-        if q < 8:
-            src = fo.at[(z + 16 - q) % 16]
-            send_right(src, src, br_send.at[q], br_recv.at[q])
+            take(fo.at[(z + q) % 16, w], bl_recv.at[q - 1, u])
         if q < 7:
-            src = fo.at[(z + q) % 16]
-            send_left(src, src, bl_send.at[q], bl_recv.at[q])
-
-    ring_sum(1)
-
-    for i in range(4):
-        part = nn(sall[i * 128 : (i + 1) * 128, 0:384], wsg[...]).astype(BF)
-        dxp[0, i] = part[:, 0:384]
-        dxp[1, i] = part[:, 256:640]
-    dx_sib = pltpu.make_async_remote_copy(
-        dxp.at[oc], dxs, ds_send, ds_recv, device_id=(z, loc(x, oc), y), device_id_type=MESH
-    )
-    dx_sib.start()
-
-    ring_sum(2)
+            src = fo.at[(z + q) % 16, w]
+            send_left(src, src, bl_send.at[q, u], bl_recv.at[q, u])
 
     def unpack(k):
         a = 8 - k
@@ -480,7 +409,7 @@
                         ).start()
 
     def dx_out():
-        dx_sib.wait_recv()
+        take(dxs, ds_recv)
         for i in range(4):
             own = jnp.logical_and(x == y, y == i)
             dxf[i] = (dxp[c, i].astype(F32) + dxs[i].astype(F32)).astype(BF)
@@ -496,52 +425,12 @@
                     device_id=(z, loc(y, c), i), device_id_type=MESH,
                 ).start()
 
-    for k in range(4):
-        unpack(k)
-        if k >= 1:
-            forward(k - 1)
-        if k >= 2:
-            across(k - 2)
-    ring_sum(3)
-    for k in range(4, 8):
-        unpack(k)
-        forward(k - 1)
-        across(k - 2)
-        if k % 2:
-            ring_sum(4 + (k - 5) // 2)
-    for k in range(4):
-        settle(k)
-    half(0)
-    ring_sum(6)
-    forward(7)
-    across(6)
-    reduce_pair(0)
-    across(7)
-    ring_sum(7)
-    for k in range(4, 8):
-        settle(k)
-    half(1)
-    ring_sum(8)
-    give_back(0)
-    reduce_pair(1)
-    ring_sum(9)
-    dx_out()
-    ring_sum(10)
-    give_back(1)
-
-    def weight_grads(i, _):
-        cols = pl.ds(pl.multiple_of(i * 640, 128), 640)
-        g2 = tn(dab[...], xf[:, cols])
-        neg_ref[0, :, cols] = g2[0:96].astype(BF)
-        neu_ref[0, :, cols] = g2[96:192].astype(BF)
-        ned_ref[0, :, cols] = tn(hq[...], df[:, cols]).astype(BF)
-        return 0
-
-    lax.fori_loop(0, 2, weight_grads, 0)
-    ring_sum(11)
-    lax.fori_loop(2, 4, weight_grads, 0)
-    ring_sum(12)
-
+    for i in range(4):
+        take(xs.at[i, c], tok_recv.at[i])
+        pltpu.make_async_remote_copy(
+            xs.at[i, c], xs.at[i, c], tsib_send.at[i], tsib_recv.at[i],
+            device_id=(z, loc(x, oc), y), device_id_type=MESH,
+        ).start()
     jc = iota((128, 1024), 1)
     jr = jc & 15
     jg = lax.shift_right_arithmetic(jc, 4) * 6
@@ -555,7 +444,7 @@
     for kk in range(1, 6):
         hit = jnp.logical_or(hit, code == pos[:, kk : kk + 1])
         hit2 = jnp.logical_or(hit2, code + 3 == pos[:, kk : kk + 1])
-    sel = jnp.concatenate(
+    selm[...] = jnp.concatenate(
         [
             one(jnp.logical_and(hit, cls_a)),
             one(jnp.logical_and(hit, cls_b)),
@@ -565,11 +454,140 @@
         axis=0,
     )
     grow = one(jnp.logical_and(iota((64, 1024), 1) == iota((64, 1024), 0) * 16 + 15, True))
+    low128 = lane < 64
+    for i in range(4):
+        take(xs.at[i, oc], tsib_recv.at[i])
+        te = xs[i, 0]
+        to = xs[i, 1]
+        te_t = te[:, 256:384].astype(F32)
+        to_t = to[:, 256:384].astype(F32)
+        rows = pl.ds(i * 128, 128)
+        xa[rows, 0:256] = te[:, 0:256]
+        xa[rows, 256:384] = jnp.where(low128, te_t, to_t).astype(BF)
+        xa[rows, 384:640] = to[:, 0:256]
+        da[rows, 0:256] = te[:, 384:640]
+        da[rows, 256:384] = jnp.where(low128, pltpu.roll(te_t, 64, 1), pltpu.roll(to_t, 64, 1)).astype(BF)
+        da[rows, 384:640] = to[:, 384:640]
+    for i in range(4):
+        rows = pl.ds(i * 128, 128)
+        sp[i, :, 0:384] = nt(xa[rows, :], wsg[...]).astype(BF)
+        sp[i, :, 384:576] = nt(da[rows, :], sd_ref[...]).astype(BF)
+        sp[i, :, 576:640] = jnp.zeros((128, 64), BF)
+    for o in range(1, 4):
+        to_y = (y + o) % 4
+        pltpu.make_async_remote_copy(
+            sp.at[to_y], r2.at[y], y_send.at[o], y_recv.at[o],
+            device_id=(z, l, to_y), device_id_type=MESH,
+        ).start()
+    r2[y] = sp[y]
+    unpack(0)
+    unpack(1)
+    forward(0)
+    unpack(2)
+    forward(1)
+    across(0)
+    unpack(3)
+    forward(2)
+    across(1)
+
+    for o in range(1, 4):
+        take(r2.at[(y + 4 - o) % 4], y_recv.at[o])
+    tot = r2[0].astype(F32) + r2[1].astype(F32) + r2[2].astype(F32) + r2[3].astype(F32)
+    sa = tot[:, 0:192]
+    sb = tot[:, 192:384]
+    se = tot[:, 384:576]
+    sig = 1.0 / (1.0 + jnp.exp(-sa))
+    sil = sa * sig
+    sdall[y] = jnp.concatenate(
+        [
+            se * sb * sig * (1.0 + sa * (1.0 - sig)),
+            se * sil,
+            sil * sb,
+            jnp.zeros((128, 64), F32),
+        ],
+        axis=1,
+    ).astype(BF)
+    for o in range(1, 4):
+        pltpu.make_async_remote_copy(
+            sdall.at[y], sdall.at[y], y2_send.at[o], y2_recv.at[o],
+            device_id=(z, l, (y + o) % 4), device_id_type=MESH,
+        ).start()
+    unpack(4)
+    forward(3)
+    across(2)
+    unpack(5)
+    forward(4)
+    across(3)
+
+    for o in range(1, 4):
+        take(sdall.at[(y + 4 - o) % 4], y2_recv.at[o])
+    sall = sdall[...].reshape(512, 640)
+    for t in range(5):
+        cols = slice(t * 128, (t + 1) * 128)
+        g2 = tn(sall[:, 0:384], xa[:, cols])
+        g1 = tn(sall[:, 384:640], da[:, cols])
+        gp[t * 3] = g2[0:192].astype(BF)
+        gp[t * 3 + 1] = g2[192:384].astype(BF)
+        gp[t * 3 + 2] = g1[0:192].astype(BF)
+    gp[15] = jnp.zeros((192, 128), BF)
+
+    ring_sum(1)
+    unpack(6)
+    forward(5)
+    across(4)
+    unpack(7)
+    forward(6)
+    across(5)
+    ring_sum(2)
+    for k in range(4):
+        settle(k)
+    half(0)
+    ring_sum(3)
+    forward(7)
+    across(6)
+    across(7)
+    ring_sum(4)
+    reduce_pair(0)
+    for k in range(4, 8):
+        settle(k)
+    ring_sum(5)
+    half(1)
+    ring_sum(6)
+    give_back(0)
+    ring_sum(7)
+    reduce_pair(1)
+    ring_sum(8)
+    for i in range(4):
+        part = nn(sall[i * 128 : (i + 1) * 128, 0:384], wsg[...]).astype(BF)
+        dxp[0, i] = part[:, 0:384]
+        dxp[1, i] = part[:, 256:640]
+    pltpu.make_async_remote_copy(
+        dxp.at[oc], dxs, ds_send, ds_recv, device_id=(z, loc(x, oc), y), device_id_type=MESH
+    ).start()
+
+    ring_sum(9)
+    give_back(1)
+    ring_sum(10)
+    dx_out()
+    ring_sum(11)
+
+    def weight_grads(i, _):
+        cols = pl.ds(pl.multiple_of(i * 640, 128), 640)
+        g2 = tn(dab[...], xf[:, cols])
+        neg_ref[0, :, cols] = g2[0:96].astype(BF)
+        neu_ref[0, :, cols] = g2[96:192].astype(BF)
+        ned_ref[0, :, cols] = tn(hq[...], df[:, cols]).astype(BF)
+        return 0
+
+    lax.fori_loop(0, 2, weight_grads, 0)
+    ring_sum(12)
+    lax.fori_loop(2, 4, weight_grads, 0)
+
     ring_sum(13)
 
     take(back, b_recv)
     rows = back[...].reshape(1024, 128)
-    got = nn(sel, rows)
+    got = nn(selm[...], rows)
     gates = nn(grow, rows).astype(BF)
     lane64 = iota((128, 64), 1)
     acc = jnp.zeros((128, 128), F32)
@@ -577,7 +595,7 @@
         gk = nn(one(lane64 == ex[:, kk : kk + 1]), gates)
         gk = jnp.sum(jnp.where(lane == rs[:, kk : kk + 1], gk, 0.0), axis=1, keepdims=True)
         acc = jnp.where(lane == kk, gk, acc)
-    gg_ref[...] = acc[:, 0:6]
+    gg_ref[...] = acc.T[0:6, :]
     ring_sum(14)
     for i in range(4):
         take(dxr.at[i], dx_recv.at[i])
@@ -585,7 +603,7 @@
     tl = got[256:384, 0:64] + got[384:512, 64:128]
     evn = jnp.concatenate([m[:, 0:128] + got[0:128], m[:, 128:256] + got[128:256], m[:, 256:320] + tl], axis=1)
     od = jnp.concatenate([m[:, 64:128] + tl, m[:, 128:256] + got[0:128], m[:, 256:384] + got[128:256]], axis=1)
-    gx_ref[...] = jnp.where(is_even, evn, od).astype(BF)
+    gx_ref[...] = tn(jnp.where(is_even, evn, od).astype(BF), eye).astype(BF)
 
     ring_sum(15)
     ring_sum(16)
@@ -617,7 +635,7 @@
     for o in range(1, 4):
         take(sp.at[0], y_send.at[o])
         take(sdall.at[0], y2_send.at[o])
-    dx_sib.wait_send()
+    take(dxs, ds_send)
     for k in range(8):
         for n in range(3):
             take(rall.at[0, 0, k], ag_send.at[k, n])
@@ -628,20 +646,35 @@
             take(s1.at[h, 0], c_send.at[h, o])
         for o in range(1, 4):
             take(s2.at[h, 0], r_send.at[h, o])
-    for q in range(8):
-        take(arr.at[0], rr_send.at[q])
-        take(fo.at[0], br_send.at[q])
-    for q in range(7):
-        take(arl.at[0], rl_send.at[q])
-        take(fo.at[0], bl_send.at[q])
+    for u in range(2):
+        w = pl.ds(u * 96, 96)
+        for q in range(8):
+            take(arr.at[0, w], rr_send.at[q, u])
+            take(fo.at[0, w], br_send.at[q, u])
+        for q in range(7):
+            take(arl.at[0, w], rl_send.at[q, u])
+            take(fo.at[0, w], bl_send.at[q, u])
+
+
+def hand_over(*refs):
+    held, came, left = refs[16:24], refs[24], refs[25]
+    inward = [pltpu.make_async_copy(refs[i], held[i], came.at[i]) for i in range(8)]
+    outward = [pltpu.make_async_copy(held[i], refs[8 + i], left.at[i]) for i in range(8)]
+    for copy in inward:
+        copy.start()
+    for i in range(8):
+        inward[i].wait()
+        outward[i].start()
+    for copy in outward:
+        copy.wait()
 
 
 def on_device(*args):
     sem = pltpu.SemaphoreType.DMA
     vm = pltpu.VMEM
     out_shape = (
-        jax.ShapeDtypeStruct((128, 320), BF),
-        jax.ShapeDtypeStruct((128, 6), F32),
+        jax.ShapeDtypeStruct((320, 128), BF),
+        jax.ShapeDtypeStruct((6, 128), F32),
         jax.ShapeDtypeStruct((192, 640), BF),
         jax.ShapeDtypeStruct((192, 640), BF),
         jax.ShapeDtypeStruct((192, 640), BF),
@@ -685,15 +718,17 @@
         vm((8, 192, 128), BF),
         vm((7, 192, 128), BF),
         vm((16, 192, 128), BF),
+        vm((512, 1024), BF),
         sem((4,)), sem((4,)), sem((4,)), sem((4,)), sem, sem((8,)),
         sem((8, 3)), sem((8, 3)), sem((8, 4)), sem((8, 4)),
         sem((4,)), sem((4,)), sem((4,)), sem((4,)),
         sem, sem, sem((4,)), sem((4,)),
-        sem((8,)), sem((8,)), sem((7,)), sem((7,)),
-        sem((8,)), sem((8,)), sem((7,)), sem((7,)),
+        sem((8, 2)), sem((8, 2)), sem((7, 2)), sem((7, 2)),
+        sem((8, 2)), sem((8, 2)), sem((7, 2)), sem((7, 2)),
         sem((2, 4)), sem((2, 4)), sem((2, 4)), sem((2, 4)), sem, sem,
     ]
-    return pl.pallas_call(
+    x, dy, gv, re, rs = [v.T for v in args[:5]]
+    outs = pl.pallas_call(
         kernel,
         out_shape=out_shape,
         in_specs=[pl.BlockSpec(memory_space=pltpu.VMEM)] * 11,
@@ -703,7 +738,17 @@
             collective_id=0, has_side_effects=True, vmem_limit_bytes=56 * 1024 * 1024
         ),
         cost_estimate=pl.CostEstimate(flops=3_000_000_000, bytes_accessed=6_000_000, transcendentals=100_000),
-    )(*args)
+    )(x, dy, gv, re, rs, *args[5:])
+    outs = pl.pallas_call(
+        hand_over,
+        out_shape=out_shape,
+        in_specs=[pl.BlockSpec(memory_space=pl.ANY)] * 8,
+        out_specs=tuple([pl.BlockSpec(memory_space=pl.ANY)] * 8),
+        scratch_shapes=[vm(v.shape, v.dtype) for v in out_shape] + [sem((8,)), sem((8,))],
+        compiler_params=pltpu.CompilerParams(vmem_limit_bytes=60 * 1024 * 1024),
+        cost_estimate=pl.CostEstimate(flops=0, bytes_accessed=5_000_000, transcendentals=0),
+    )(*outs)
+    return (outs[0].T, outs[1].T, *outs[2:])
 
 
 def solution(mesh):

time: 153 us -> 128 us (0.84)
  local copies, waits for them, and re-layouts: 13.4 us -> 0 us
  Pallas kernels: 138 us -> 127 us
    pallas_call x1, Pallas kernels: 138 us -> 124 us  [on_device(): pl.pallas_call(kernel, out_shape=out_shape, in_specs=[pl.BlockSpec(memory...]
    unnamed x31 -> x0, local copies, waits for them, and re-layouts: 10.2 us -> none
    pallas_call x2 -> x0, local copies, waits for them, and re-layouts: 3.18 us -> none  [on_device(): pl.pallas_call(kernel, out_shape=out_shape, in_specs=[pl.BlockSpec(memory...]
    pallas_call x0 -> x1, Pallas kernels: none -> 2.64 us  [on_device(): pl.pallas_call(hand_over, out_shape=out_shape, in_specs=[pl.BlockSpec(mem...]
where the time goes in v2:
time: 128 us
  Pallas kernels  127 us (99%)
    pallas_call x1, Pallas kernels, on_device(): pl.pallas_call(kernel, out_shape=out_shape, in_specs=[pl.BlockSpec(memory...  124 us
    pallas_call x1, Pallas kernels, on_device(): pl.pallas_call(hand_over, out_shape=out_shape, in_specs=[pl.BlockSpec(mem...  2.64 us

profile of v2, /device:TPU:6, one launch (start us, length us, event | category | flops | bytes accessed | tf_op | source)
XLA Modules:
  0.0 127.6 jit_solution(16002032700450053638)
XLA Ops:
  0.6 124.2 %shard_map.170 = (bf16[320,128]{1,0:T(8,128)(2,1)}, f32[6,128]{1,0:T(8,128)}, bf16[192,640]{1,0:T(8,128)(2,1)}, bf16[192,640]{1,0:T(8,128)(2,1)}, bf16[192,640]{...) custom-call(bf16[320,128]{1,0:T(8,128)(2,1)} %bitcast.7, ...), custom_call_target="tpu_custom_call" | custom-call | flops 3000000000 | bytes 6000000 | tf_op jit(solution)/shard_map/pallas_call | solution.py:731
  124.8 2.6 %shard_map.171 = (bf16[320,128]{1,0:T(8,128)(2,1)}, f32[6,128]{1,0:T(8,128)}, bf16[192,640]{1,0:T(8,128)(2,1)}, bf16[192,640]{1,0:T(8,128)(2,1)}, bf16[192,640]{...) custom-call(bf16[320,128]{1,0:T(8,128)(2,1)} %get-tuple-element.24.refs_, ...), custom_call_target="tpu_custom_call" | custom-call | bytes 5000000 | tf_op jit(solution)/shard_map/pallas_call | solution.py:742

commit v3 on v2

--- a/solution.py
+++ b/solution.py
@@ -42,11 +42,12 @@
     x_ref, dy_ref, gv_ref, re_ref, rs_ref, sg_ref, su_ref, sd_ref, eg_ref, eu_ref, ed_ref,
     gx_ref, gg_ref, gsg_ref, gsu_ref, gsd_ref, neg_ref, neu_ref, ned_ref,
     tx, pb, pr, vcat, qm, qr, rall, qv, xf, df, wgu, dab, hq, pkb, s1, s2, s3, ret, back, rd,
-    xs, xa, da, wsg, sp, r2, sdall, dxp, dxs, dxf, dxr, gp, arr, arl, fo, selm,
+    xs, xa, da, wsg, sp, r2, sdall, dxp, dxs, dxf, dxr, gp, ra, ro, la, lo, fo, selm,
     tok_send, tok_recv, tsib_send, tsib_recv, disp_send, disp_recv,
     ag_send, ag_recv, as_send, as_recv, y_send, y_recv, y2_send, y2_recv,
-    ds_send, ds_recv, dx_send, dx_recv, rr_send, rr_recv, rl_send, rl_recv,
-    br_send, br_recv, bl_send, bl_recv, c_send, c_recv, r_send, r_recv, b_send, b_recv,
+    ds_send, ds_recv, dx_send, dx_recv, ra_send, ra_recv, ro_send, ro_recv,
+    la_send, la_recv, lo_send, lo_recv, be_send, be_recv, bo_send, bo_recv,
+    le_send, le_recv, ll_send, ll_recv, c_send, c_recv, r_send, r_recv, b_send, b_recv,
 ):
     z = lax.axis_index("node")
     y = lax.axis_index("dp")
@@ -199,53 +200,74 @@
     low48 = lane48 < 64
     c48 = row48 - sixth(row48) * 6
 
-    zr = (z + 1) % 16
-    zl = (z + 15) % 16
-
-    def send_right(src, dst, ss, rsem):
+    def hop(src, dst, ss, rsem, by):
         pltpu.make_async_remote_copy(
-            src, dst, ss, rsem, device_id=(zr, l, y), device_id_type=MESH
+            src, dst, ss, rsem, device_id=((z + 16 + by) % 16, l, y), device_id_type=MESH
         ).start()
 
-    def send_left(src, dst, ss, rsem):
-        pltpu.make_async_remote_copy(
-            src, dst, ss, rsem, device_id=(zl, l, y), device_id_type=MESH
-        ).start()
-
-    def ring_sum(s):
+    def ring(s):
         for u in range(2):
             ring_part(s, u, pl.ds(u * 96, 96))
 
+    def term(d, w):
+        return gp[(z + 16 + d) % 16, w].astype(F32)
+
+    def odd_right(i, u, w):
+        hop(gp.at[(z + 7 - 2 * i) % 16, w], ro.at[i, w], ro_send.at[i, u], ro_recv.at[i, u], 1)
+
+    def odd_left(i, u, w):
+        hop(gp.at[(z + 9 + 2 * i) % 16, w], lo.at[i, w], lo_send.at[i, u], lo_recv.at[i, u], -1)
+
     def ring_part(s, u, w):
-        if s == 1:
-            send_right(gp.at[(z + 8) % 16, w], arr.at[0, w], rr_send.at[0, u], rr_recv.at[0, u])
-            send_left(gp.at[(z + 9) % 16, w], arl.at[0, w], rl_send.at[0, u], rl_recv.at[0, u])
-            return
-        if s <= 8:
-            q = s - 2
-            take(arr.at[q, w], rr_recv.at[q, u])
-            arr[q, w] = (arr[q, w].astype(F32) + gp[(z + 9 - s) % 16, w].astype(F32)).astype(BF)
-            send_right(arr.at[q, w], arr.at[q + 1, w], rr_send.at[q + 1, u], rr_recv.at[q + 1, u])
-            if s <= 7:
-                take(arl.at[q, w], rl_recv.at[q, u])
-                arl[q, w] = (arl[q, w].astype(F32) + gp[(z + 8 + s) % 16, w].astype(F32)).astype(BF)
-                send_left(arl.at[q, w], arl.at[q + 1, w], rl_send.at[q + 1, u], rl_recv.at[q + 1, u])
-            return
-        if s == 9:
-            take(arr.at[7, w], rr_recv.at[7, u])
-            take(arl.at[6, w], rl_recv.at[6, u])
-            fo[z, w] = (gp[z, w].astype(F32) + arr[7, w].astype(F32) + arl[6, w].astype(F32)).astype(BF)
-        q = s - 9
-        if q > 0 and q <= 8:
-            take(fo.at[(z + 16 - q) % 16, w], br_recv.at[q - 1, u])
-        if q < 8:
-            src = fo.at[(z + 16 - q) % 16, w]
-            send_right(src, src, br_send.at[q, u], br_recv.at[q, u])
-        if q > 0 and q <= 7:
-            take(fo.at[(z + q) % 16, w], bl_recv.at[q - 1, u])
-        if q < 7:
-            src = fo.at[(z + q) % 16, w]
-            send_left(src, src, bl_send.at[q, u], bl_recv.at[q, u])
+        if s == 0:
+            hop(gp.at[(z + 8) % 16, w], ra.at[0, w], ra_send.at[0, u], ra_recv.at[0, u], 2)
+            odd_left(0, u, w)
+            odd_right(0, u, w)
+            odd_left(1, u, w)
+            odd_right(1, u, w)
+        elif s <= 3:
+            q = s - 1
+            take(lo.at[q, w], lo_recv.at[q, u])
+            v = lo[q, w].astype(F32) + term(2 * s - 8, w)
+            if s > 1:
+                take(la.at[s - 2, w], la_recv.at[s - 2, u])
+                v = v + la[s - 2, w].astype(F32)
+            lo[q, w] = v.astype(BF)
+            hop(lo.at[q, w], la.at[q, w], la_send.at[q, u], la_recv.at[q, u], -2)
+            take(ra.at[q, w], ra_recv.at[q, u])
+            take(ro.at[q, w], ro_recv.at[q, u])
+            v = ra[q, w].astype(F32) + ro[q, w].astype(F32) + term(8 - 2 * s, w)
+            ra[q, w] = v.astype(BF)
+            hop(ra.at[q, w], ra.at[s, w], ra_send.at[s, u], ra_recv.at[s, u], 2)
+            if s < 3:
+                odd_left(s + 1, u, w)
+                odd_right(s + 1, u, w)
+        elif s <= 7:
+            p = s - 4
+            if p == 0:
+                take(la.at[2, w], la_recv.at[2, u])
+                take(lo.at[3, w], lo_recv.at[3, u])
+                take(ra.at[3, w], ra_recv.at[3, u])
+                take(ro.at[3, w], ro_recv.at[3, u])
+                v = term(0, w) + ra[3, w].astype(F32) + ro[3, w].astype(F32)
+                v = v + la[2, w].astype(F32) + lo[3, w].astype(F32)
+                fo[z, w] = v.astype(BF)
+            src = fo.at[(z + 16 - 2 * p) % 16, w]
+            if p:
+                take(src, be_recv.at[p - 1, u])
+            hop(src, src, be_send.at[p, u], be_recv.at[p, u], 2)
+            src2 = fo.at[(z + 2 * p) % 16, w]
+            if p:
+                take(src2, le_recv.at[p - 1, u])
+            if p < 3:
+                hop(src2, src2, le_send.at[p, u], le_recv.at[p, u], -2)
+            hop(src, src, bo_send.at[p, u], bo_recv.at[p, u], 1)
+            hop(src2, src2, ll_send.at[p, u], ll_recv.at[p, u], -1)
+        else:
+            take(fo.at[(z + 8) % 16, w], be_recv.at[3, u])
+            for p in range(4):
+                take(fo.at[(z + 15 - 2 * p) % 16, w], bo_recv.at[p, u])
+                take(fo.at[(z + 1 + 2 * p) % 16, w], ll_recv.at[p, u])
 
     def unpack(k):
         a = 8 - k
@@ -425,12 +447,49 @@
                     device_id=(z, loc(y, c), i), device_id_type=MESH,
                 ).start()
 
-    for i in range(4):
+    low128 = lane < 64
+
+    def group_in(o):
+        i = (y + o) % 4
         take(xs.at[i, c], tok_recv.at[i])
         pltpu.make_async_remote_copy(
             xs.at[i, c], xs.at[i, c], tsib_send.at[i], tsib_recv.at[i],
             device_id=(z, loc(x, oc), y), device_id_type=MESH,
         ).start()
+
+    def group_forward(o):
+        i = (y + o) % 4
+        take(xs.at[i, oc], tsib_recv.at[i])
+        te = xs[i, 0]
+        to = xs[i, 1]
+        te_t = te[:, 256:384].astype(F32)
+        to_t = to[:, 256:384].astype(F32)
+        rows = pl.ds(pl.multiple_of(i * 128, 128), 128)
+        xa[rows, 0:256] = te[:, 0:256]
+        xa[rows, 256:384] = jnp.where(low128, te_t, to_t).astype(BF)
+        xa[rows, 384:640] = to[:, 0:256]
+        da[rows, 0:256] = te[:, 384:640]
+        da[rows, 256:384] = jnp.where(low128, pltpu.roll(te_t, 64, 1), pltpu.roll(to_t, 64, 1)).astype(BF)
+        da[rows, 384:640] = to[:, 384:640]
+        sp[i, :, 0:384] = nt(xa[rows, :], wsg[...]).astype(BF)
+        sp[i, :, 384:576] = nt(da[rows, :], sd_ref[...]).astype(BF)
+        sp[i, :, 576:640] = jnp.zeros((128, 64), BF)
+        if o:
+            pltpu.make_async_remote_copy(
+                sp.at[i], r2.at[y], y_send.at[o], y_recv.at[o],
+                device_id=(z, l, i), device_id_type=MESH,
+            ).start()
+        else:
+            r2[y] = sp[y]
+
+    group_in(1)
+    group_in(3)
+    group_forward(1)
+    group_in(2)
+    group_forward(3)
+    group_in(0)
+    group_forward(2)
+    group_forward(0)
     jc = iota((128, 1024), 1)
     jr = jc & 15
     jg = lax.shift_right_arithmetic(jc, 4) * 6
@@ -454,32 +513,6 @@
         axis=0,
     )
     grow = one(jnp.logical_and(iota((64, 1024), 1) == iota((64, 1024), 0) * 16 + 15, True))
-    low128 = lane < 64
-    for i in range(4):
-        take(xs.at[i, oc], tsib_recv.at[i])
-        te = xs[i, 0]
-        to = xs[i, 1]
-        te_t = te[:, 256:384].astype(F32)
-        to_t = to[:, 256:384].astype(F32)
-        rows = pl.ds(i * 128, 128)
-        xa[rows, 0:256] = te[:, 0:256]
-        xa[rows, 256:384] = jnp.where(low128, te_t, to_t).astype(BF)
-        xa[rows, 384:640] = to[:, 0:256]
-        da[rows, 0:256] = te[:, 384:640]
-        da[rows, 256:384] = jnp.where(low128, pltpu.roll(te_t, 64, 1), pltpu.roll(to_t, 64, 1)).astype(BF)
-        da[rows, 384:640] = to[:, 384:640]
-    for i in range(4):
-        rows = pl.ds(i * 128, 128)
-        sp[i, :, 0:384] = nt(xa[rows, :], wsg[...]).astype(BF)
-        sp[i, :, 384:576] = nt(da[rows, :], sd_ref[...]).astype(BF)
-        sp[i, :, 576:640] = jnp.zeros((128, 64), BF)
-    for o in range(1, 4):
-        to_y = (y + o) % 4
-        pltpu.make_async_remote_copy(
-            sp.at[to_y], r2.at[y], y_send.at[o], y_recv.at[o],
-            device_id=(z, l, to_y), device_id_type=MESH,
-        ).start()
-    r2[y] = sp[y]
     unpack(0)
     unpack(1)
     forward(0)
@@ -531,32 +564,30 @@
         gp[t * 3 + 2] = g1[0:192].astype(BF)
     gp[15] = jnp.zeros((192, 128), BF)
 
-    ring_sum(1)
+    ring(0)
     unpack(6)
     forward(5)
     across(4)
     unpack(7)
     forward(6)
     across(5)
-    ring_sum(2)
+    ring(1)
     for k in range(4):
         settle(k)
     half(0)
-    ring_sum(3)
+    ring(2)
     forward(7)
     across(6)
     across(7)
-    ring_sum(4)
     reduce_pair(0)
+    ring(3)
     for k in range(4, 8):
         settle(k)
-    ring_sum(5)
     half(1)
-    ring_sum(6)
+    ring(4)
     give_back(0)
-    ring_sum(7)
     reduce_pair(1)
-    ring_sum(8)
+    ring(5)
     for i in range(4):
         part = nn(sall[i * 128 : (i + 1) * 128, 0:384], wsg[...]).astype(BF)
         dxp[0, i] = part[:, 0:384]
@@ -565,11 +596,9 @@
         dxp.at[oc], dxs, ds_send, ds_recv, device_id=(z, loc(x, oc), y), device_id_type=MESH
     ).start()
 
-    ring_sum(9)
     give_back(1)
-    ring_sum(10)
+    ring(6)
     dx_out()
-    ring_sum(11)
 
     def weight_grads(i, _):
         cols = pl.ds(pl.multiple_of(i * 640, 128), 640)
@@ -580,10 +609,9 @@
         return 0
 
     lax.fori_loop(0, 2, weight_grads, 0)
-    ring_sum(12)
+    ring(7)
     lax.fori_loop(2, 4, weight_grads, 0)
 
-    ring_sum(13)
 
     take(back, b_recv)
     rows = back[...].reshape(1024, 128)
@@ -596,7 +624,6 @@
         gk = jnp.sum(jnp.where(lane == rs[:, kk : kk + 1], gk, 0.0), axis=1, keepdims=True)
         acc = jnp.where(lane == kk, gk, acc)
     gg_ref[...] = acc.T[0:6, :]
-    ring_sum(14)
     for i in range(4):
         take(dxr.at[i], dx_recv.at[i])
     m = dxr[0].astype(F32) + dxr[1].astype(F32) + dxr[2].astype(F32) + dxr[3].astype(F32)
@@ -605,9 +632,7 @@
     od = jnp.concatenate([m[:, 64:128] + tl, m[:, 128:256] + got[0:128], m[:, 256:384] + got[128:256]], axis=1)
     gx_ref[...] = tn(jnp.where(is_even, evn, od).astype(BF), eye).astype(BF)
 
-    ring_sum(15)
-    ring_sum(16)
-    ring_sum(17)
+    ring(8)
     for t in range(5):
         cols = slice(t * 128, (t + 1) * 128)
         gsg_ref[:, cols] = fo[t * 3]
@@ -648,12 +673,16 @@
             take(s2.at[h, 0], r_send.at[h, o])
     for u in range(2):
         w = pl.ds(u * 96, 96)
-        for q in range(8):
-            take(arr.at[0, w], rr_send.at[q, u])
-            take(fo.at[0, w], br_send.at[q, u])
-        for q in range(7):
-            take(arl.at[0, w], rl_send.at[q, u])
-            take(fo.at[0, w], bl_send.at[q, u])
+        for q in range(4):
+            take(fo.at[0, w], ra_send.at[q, u])
+            take(fo.at[0, w], ro_send.at[q, u])
+            take(fo.at[0, w], lo_send.at[q, u])
+            take(fo.at[0, w], be_send.at[q, u])
+            take(fo.at[0, w], bo_send.at[q, u])
+            take(fo.at[0, w], ll_send.at[q, u])
+        for q in range(3):
+            take(fo.at[0, w], la_send.at[q, u])
+            take(fo.at[0, w], le_send.at[q, u])
 
 
 def hand_over(*refs):
@@ -715,16 +744,20 @@
         vm((4, 128, 384), BF),
         vm((4, 128, 384), BF),
         vm((16, 192, 128), BF),
-        vm((8, 192, 128), BF),
-        vm((7, 192, 128), BF),
+        vm((4, 192, 128), BF),
+        vm((4, 192, 128), BF),
+        vm((3, 192, 128), BF),
+        vm((4, 192, 128), BF),
         vm((16, 192, 128), BF),
         vm((512, 1024), BF),
         sem((4,)), sem((4,)), sem((4,)), sem((4,)), sem, sem((8,)),
         sem((8, 3)), sem((8, 3)), sem((8, 4)), sem((8, 4)),
         sem((4,)), sem((4,)), sem((4,)), sem((4,)),
         sem, sem, sem((4,)), sem((4,)),
-        sem((8, 2)), sem((8, 2)), sem((7, 2)), sem((7, 2)),
-        sem((8, 2)), sem((8, 2)), sem((7, 2)), sem((7, 2)),
+        sem((4, 2)), sem((4, 2)), sem((4, 2)), sem((4, 2)),
+        sem((3, 2)), sem((3, 2)), sem((4, 2)), sem((4, 2)),
+        sem((4, 2)), sem((4, 2)), sem((4, 2)), sem((4, 2)),
+        sem((3, 2)), sem((3, 2)), sem((4, 2)), sem((4, 2)),
         sem((2, 4)), sem((2, 4)), sem((2, 4)), sem((2, 4)), sem, sem,
     ]
     x, dy, gv, re, rs = [v.T for v in args[:5]]

time: 128 us -> 118 us (0.922)
  the two profiles are of different devices: /device:TPU:6 before, /device:TPU:57 now
where the time goes in v3:
time: 118 us
  Pallas kernels  118 us (100%)
    pallas_call x1, Pallas kernels, on_device(): pl.pallas_call(kernel, out_shape=out_shape, in_specs=[pl.BlockSpec(memory...  115 us
    pallas_call x1, Pallas kernels, on_device(): pl.pallas_call(hand_over, out_shape=out_shape, in_specs=[pl.BlockSpec(mem...  2.64 us

profile of v3, /device:TPU:57, one launch (start us, length us, event | category | flops | bytes accessed | tf_op | source)
XLA Modules:
  0.0 118.3 jit_solution(14535310893817403252)
XLA Ops:
  0.6 114.9 %shard_map.170 = (bf16[320,128]{1,0:T(8,128)(2,1)}, f32[6,128]{1,0:T(8,128)}, bf16[192,640]{1,0:T(8,128)(2,1)}, bf16[192,640]{1,0:T(8,128)(2,1)}, bf16[192,640]{...) custom-call(bf16[320,128]{1,0:T(8,128)(2,1)} %bitcast.7, ...), custom_call_target="tpu_custom_call" | custom-call | flops 3000000000 | bytes 6000000 | tf_op jit(solution)/shard_map/pallas_call | solution.py:764
  115.5 2.6 %shard_map.171 = (bf16[320,128]{1,0:T(8,128)(2,1)}, f32[6,128]{1,0:T(8,128)}, bf16[192,640]{1,0:T(8,128)(2,1)}, bf16[192,640]{1,0:T(8,128)(2,1)}, bf16[192,640]{...) custom-call(bf16[320,128]{1,0:T(8,128)(2,1)} %get-tuple-element.24.refs_, ...), custom_call_target="tpu_custom_call" | custom-call | bytes 5000000 | tf_op jit(solution)/shard_map/pallas_call | solution.py:775

commit v4 on v3

--- a/solution.py
+++ b/solution.py
@@ -572,6 +572,14 @@
     forward(6)
     across(5)
     ring(1)
+    for i in range(4):
+        part = nn(sall[i * 128 : (i + 1) * 128, 0:384], wsg[...]).astype(BF)
+        dxp[0, i] = part[:, 0:384]
+        dxp[1, i] = part[:, 256:640]
+    pltpu.make_async_remote_copy(
+        dxp.at[oc], dxs, ds_send, ds_recv, device_id=(z, loc(x, oc), y), device_id_type=MESH
+    ).start()
+
     for k in range(4):
         settle(k)
     half(0)
@@ -587,19 +595,7 @@
     ring(4)
     give_back(0)
     reduce_pair(1)
-    ring(5)
-    for i in range(4):
-        part = nn(sall[i * 128 : (i + 1) * 128, 0:384], wsg[...]).astype(BF)
-        dxp[0, i] = part[:, 0:384]
-        dxp[1, i] = part[:, 256:640]
-    pltpu.make_async_remote_copy(
-        dxp.at[oc], dxs, ds_send, ds_recv, device_id=(z, loc(x, oc), y), device_id_type=MESH
-    ).start()
-
-    give_back(1)
-    ring(6)
     dx_out()
-
     def weight_grads(i, _):
         cols = pl.ds(pl.multiple_of(i * 640, 128), 640)
         g2 = tn(dab[...], xf[:, cols])
@@ -609,9 +605,13 @@
         return 0
 
     lax.fori_loop(0, 2, weight_grads, 0)
+    ring(5)
+    lax.fori_loop(2, 4, weight_grads, 0)
+
+
+    give_back(1)
+    ring(6)
     ring(7)
-    lax.fori_loop(2, 4, weight_grads, 0)
-
 
     take(back, b_recv)
     rows = back[...].reshape(1024, 128)

time: 118 us -> 112 us (0.949)
  the two profiles are of different devices: /device:TPU:57 before, /device:TPU:6 now
where the time goes in v4:
time: 112 us; the launch traced here: 110 us
  Pallas kernels  109 us (97%)
    pallas_call x1, Pallas kernels, on_device(): pl.pallas_call(kernel, out_shape=out_shape, in_specs=[pl.BlockSpec(memory...  106 us
    pallas_call x1, Pallas kernels, on_device(): pl.pallas_call(hand_over, out_shape=out_shape, in_specs=[pl.BlockSpec(mem...  2.64 us

profile of v4, /device:TPU:6, one launch (start us, length us, event | category | flops | bytes accessed | tf_op | source)
XLA Modules:
  0.0 109.9 jit_solution(8387211035626394353)
XLA Ops:
  0.6 106.4 %shard_map.170 = (bf16[320,128]{1,0:T(8,128)(2,1)}, f32[6,128]{1,0:T(8,128)}, bf16[192,640]{1,0:T(8,128)(2,1)}, bf16[192,640]{1,0:T(8,128)(2,1)}, bf16[192,640]{...) custom-call(bf16[320,128]{1,0:T(8,128)(2,1)} %bitcast.7, ...), custom_call_target="tpu_custom_call" | custom-call | flops 3000000000 | bytes 6000000 | tf_op jit(solution)/shard_map/pallas_call | solution.py:764
  107.1 2.6 %shard_map.171 = (bf16[320,128]{1,0:T(8,128)(2,1)}, f32[6,128]{1,0:T(8,128)}, bf16[192,640]{1,0:T(8,128)(2,1)}, bf16[192,640]{1,0:T(8,128)(2,1)}, bf16[192,640]{...) custom-call(bf16[320,128]{1,0:T(8,128)(2,1)} %get-tuple-element.24.refs_, ...), custom_call_target="tpu_custom_call" | custom-call | bytes 5000000 | tf_op jit(solution)/shard_map/pallas_call | solution.py:775
